TPU v7x, 32 devices: a whole 2x2x4 slice. The times are simulated.
32 devices in a mesh: head: 2 (over y), blk: 16 (over z, x, core).
Axes of the slice: x: 2, y: 2, z: 4, core: 2. Of those that a mesh axis runs over, the one named last changes fastest.
Arguments:
- hidden_in: float32 [8192, 1, 768], P(('head', 'blk')), may hold values from -6 to 6
- w_query: bfloat16 [768, 768], P(('head', 'blk')), may hold values from -0.21875 to 0.21875
- w_key: bfloat16 [768, 768], P(('head', 'blk')), may hold values from -0.21875 to 0.21875
- w_value: bfloat16 [768, 768], P(('head', 'blk')), may hold values from -0.21875 to 0.21875
- w_out: bfloat16 [768, 768], P(('head', 'blk')), may hold values from -6 to 6
- norm_attn: bfloat16 [768], P(('head', 'blk')), may hold values from 0.5 to 1.5
- norm_ffn: bfloat16 [768], P(('head', 'blk')), may hold values from 0.5 to 1.5
- w_router: bfloat16 [768, 16], P(('head', 'blk')), may hold values from -0.21875 to 0.21875
- shared_gate: bfloat16 [768, 2048], P(('head', 'blk')), may hold values from -0.21875 to 0.21875
- shared_up: bfloat16 [768, 2048], P(('head', 'blk')), may hold values from -0.21875 to 0.21875
- shared_down: bfloat16 [2048, 768], P(('head', 'blk')), may hold values from -0.125 to 0.125
- expert_gate: bfloat16 [768, 32768], P(None, ('head', 'blk')), may hold values from -0.21875 to 0.21875
- expert_up: bfloat16 [768, 32768], P(None, ('head', 'blk')), may hold values from -0.21875 to 0.21875
- expert_down: bfloat16 [32768, 768], P(('head', 'blk')), may hold values from -0.125 to 0.125
- teacher: float32 [8192, 1, 768], P(('head', 'blk')), may hold values from -5 to 5
- routes: int32 [8192, 1, 2], P(('head', 'blk')), may hold values from 0 to 15, all different within a row; in each aligned block of 256 rows (0 to 255, 256 to 511, ..., all dimensions but the last counted through in order) at most 64 rows name the same one
- cont_lengths: int32 [1, 8], replicated, may hold values from 256 to 768, as said below
- valid_mask: int32 [8192, 1], P(('head', 'blk')), may hold values from 0 to 1, as said below
Outputs:
- layer_out: float32 [8192, 1, 768], P(('head', 'blk'))
- input_grad: float32 [8192, 1, 768], P(('head', 'blk'))
- loss_value: float32 [], replicated
- grad_query: float32 [768, 768], P(('head', 'blk'))
- grad_key: float32 [768, 768], P(('head', 'blk'))
- grad_value: float32 [768, 768], P(('head', 'blk'))
- grad_out: float32 [768, 768], P(('head', 'blk'))
- grad_norm_attn: float32 [768], P(('head', 'blk'))
- grad_norm_ffn: float32 [768], P(('head', 'blk'))
- grad_router: float32 [768, 16], P(('head', 'blk'))
- grad_shared_gate: float32 [768, 2048], P(('head', 'blk'))
- grad_shared_up: float32 [768, 2048], P(('head', 'blk'))
- grad_shared_down: float32 [2048, 768], P(('head', 'blk'))
- grad_expert_gate: float32 [768, 32768], P(None, ('head', 'blk'))
- grad_expert_up: float32 [768, 32768], P(None, ('head', 'blk'))
- grad_expert_down: float32 [32768, 768], P(('head', 'blk'))
Inputs may be any that keep to these rules, and one draw needn't show every extreme that they name: `routes`: the 2 experts of a token differ; among the tokens of one device (aligned blocks of 256 tokens, positions then groups) no expert is named more than 64 times, a bound that some block reaches. `cont_lengths`: a group's prompt fills its positions 0 to 4095 and its 8 continuations follow in order with these lengths, which add up to 4096 in each group. `valid_mask`: position 0 of every group is valid.
All inputs are finite; a program needn't handle non-finite values.
Results may differ from a plain program's by a relative error of at most 0.039.
Values may be sent and summed in bfloat16 or wider, within the bound.
A program may use at most 768 MiB of HBM per device.

v0:
```python
import math

import jax
import jax.numpy as jnp
from jax import lax
from jax.sharding import PartitionSpec as P

HEADS = 12
HEAD_DIM = 64
EXPERTS = 16
TOP = 2
PROMPT = 4096
CAP = 64


EPSILON = 1e-06
NEGATIVE = -1e30


def apply_silu(argument):
    return argument * jax.nn.sigmoid(argument)


def silu_slope(argument):
    sigmoid_val = jax.nn.sigmoid(argument)
    return sigmoid_val * (1.0 + argument * (1.0 - sigmoid_val))


def root_norm(inputs, gain_vec):
    scaling = lax.rsqrt(jnp.mean(inputs * inputs, axis=-1, keepdims=True) + EPSILON)
    return (inputs * scaling * gain_vec, scaling)


def root_norm_back(inputs, scaling, gain_vec, upstream):
    weighted = gain_vec * upstream
    through = scaling * weighted - inputs * scaling**3 * jnp.mean(
        weighted * inputs, axis=-1, keepdims=True
    )
    return (through, jnp.sum(upstream * inputs * scaling, axis=0))


def segment_starts(positions, cont_lengths):
    run_ends = jnp.cumsum(cont_lengths, axis=1)
    begins = PROMPT + run_ends - cont_lengths
    passed = begins[None, :, :] <= positions[:, None, None]
    return jnp.max(jnp.where(passed, begins[None], 0), axis=-1)


def rotary_tables(positions, run_begin):
    relative = jnp.where(
        positions[:, None] < PROMPT, positions[:, None], PROMPT + positions[:, None] - run_begin
    )
    angle_pos = relative.astype(jnp.float32)
    half_dim = HEAD_DIM // 2
    frequency = jnp.exp(
        jnp.arange(half_dim, dtype=jnp.int32).astype(jnp.float32)
        * (-2.0 * math.log(10000.0) / HEAD_DIM)
    )
    angles = angle_pos[:, :, None, None] * frequency
    return (jnp.cos(angles), jnp.sin(angles))


def rotate(inputs, cosine_table, sine_table):
    half_dim = inputs.shape[-1] // 2
    first_half = inputs[..., :half_dim]
    second_half = inputs[..., half_dim:]
    return jnp.concatenate(
        [
            first_half * cosine_table - second_half * sine_table,
            second_half * cosine_table + first_half * sine_table,
        ],
        axis=-1,
    )


def rotate_back(upstream, cosine_table, sine_table):
    half_dim = upstream.shape[-1] // 2
    first_half = upstream[..., :half_dim]
    second_half = upstream[..., half_dim:]
    return jnp.concatenate(
        [
            first_half * cosine_table + second_half * sine_table,
            second_half * cosine_table - first_half * sine_table,
        ],
        axis=-1,
    )


def make_allowed(query_pos, query_begin, key_pos):
    causal = key_pos[None, :] <= query_pos[:, None]
    own_run = (key_pos[None, None, :] < PROMPT) | (
        key_pos[None, None, :] >= query_begin.T[:, :, None]
    )
    return causal[None] & own_run


def spread_position(global_row, rows_dev, head_count, cycle_count):
    device_blk = global_row // (head_count * rows_dev)
    within = global_row % (head_count * rows_dev)
    return (within // rows_dev * cycle_count + device_blk) * rows_dev + within % rows_dev


def forward_step(queries, query_pos, query_begin, key_place, score_scale):

    def step(fold_state, shard_piece, first_row):
        row_top, row_total, weighted_sum = fold_state
        key_part, value_part = shard_piece
        key_pos = key_place(jnp.arange(key_part.shape[0], dtype=jnp.int32))
        allowed = make_allowed(query_pos, query_begin, key_pos)[:, None]
        scores = (
            jnp.einsum("qghd,kghd->ghqk", queries, key_part, preferred_element_type=jnp.float32)
            * score_scale
        )
        scores = jnp.where(allowed, scores, NEGATIVE)
        new_top = jnp.maximum(row_top, jnp.max(scores, axis=-1))
        weights = jnp.where(allowed, jnp.exp(scores - new_top[..., None]), 0.0)
        row_total = jnp.sum(weights, axis=-1)
        weighted_sum = jnp.einsum(
            "ghqk,kghd->ghqd",
            weights.astype(jnp.bfloat16),
            value_part,
            preferred_element_type=jnp.float32,
        )
        return (new_top, row_total, weighted_sum)

    return step


def split_stats(log_total, offsets):
    pieces_list = []
    for statistic in (log_total, offsets):
        rowwise = statistic.transpose(2, 0, 1)
        leading = rowwise.astype(jnp.bfloat16)
        remainder = (rowwise - leading.astype(jnp.float32)).astype(jnp.bfloat16)
        pieces_list.append(leading)
        pieces_list.append(remainder)
    return jnp.stack(pieces_list, axis=1)


def backward_step(local_parts, query_pos, query_begin, key_place, cont_lengths, score_scale):
    queries, key_rows, value_rows, grad_heads, log_total, offsets = local_parts

    def step(fold_state, shard_piece, first_row):
        far_query, far_key, far_value, far_grad, far_stats = shard_piece
        far_pos = key_place(jnp.arange(far_key.shape[0], dtype=jnp.int32))
        allowed = make_allowed(query_pos, query_begin, far_pos)[:, None]
        scores = (
            jnp.einsum("qghd,kghd->ghqk", queries, far_key, preferred_element_type=jnp.float32)
            * score_scale
        )
        probabilities = jnp.where(allowed, jnp.exp(scores - log_total[..., None]), 0.0)
        grad_probs = jnp.einsum(
            "qghd,kghd->ghqk", grad_heads, far_value, preferred_element_type=jnp.float32
        )
        grad_scores = probabilities * (grad_probs - offsets[..., None])
        grad_query = (
            jnp.einsum(
                "ghqk,kghd->qghd",
                grad_scores.astype(jnp.bfloat16),
                far_key,
                preferred_element_type=jnp.float32,
            )
            * score_scale
        )
        far_begin = segment_starts(far_pos, cont_lengths)
        far_log = (
            far_stats[:, 0].astype(jnp.float32) + far_stats[:, 1].astype(jnp.float32)
        ).transpose(1, 2, 0)
        far_offset = (
            far_stats[:, 2].astype(jnp.float32) + far_stats[:, 3].astype(jnp.float32)
        ).transpose(1, 2, 0)
        allowed_far = make_allowed(far_pos, far_begin, query_pos)[:, None]
        scores_far = (
            jnp.einsum("pghd,kghd->ghpk", far_query, key_rows, preferred_element_type=jnp.float32)
            * score_scale
        )
        probs_far = jnp.where(allowed_far, jnp.exp(scores_far - far_log[..., None]), 0.0)
        grad_far = jnp.einsum(
            "pghd,kghd->ghpk", far_grad, value_rows, preferred_element_type=jnp.float32
        )
        grad_scores_far = probs_far * (grad_far - far_offset[..., None])
        grad_key = (
            jnp.einsum(
                "ghpk,pghd->kghd",
                grad_scores_far.astype(jnp.bfloat16),
                far_query,
                preferred_element_type=jnp.float32,
            )
            * score_scale
        )
        grad_value = jnp.einsum(
            "ghpk,pghd->kghd",
            probs_far.astype(jnp.bfloat16),
            far_grad,
            preferred_element_type=jnp.float32,
        )
        return (grad_query, grad_key, grad_value)

    return step


def to_heads(stacked):
    return lax.all_to_all(stacked, "head", split_axis=3, concat_axis=1, tiled=True)


def from_heads(stacked):
    return lax.all_to_all(stacked, "head", split_axis=1, concat_axis=3, tiled=True)


def to_experts(buffer_rows):
    return lax.all_to_all(buffer_rows, ("head", "blk"), split_axis=0, concat_axis=0, tiled=True)


def from_experts(buffer_rows):
    return lax.all_to_all(
        buffer_rows.astype(jnp.bfloat16), ("head", "blk"), split_axis=0, concat_axis=0, tiled=True
    ).astype(buffer_rows.dtype)


def on_device(
    hidden_in,
    w_query,
    w_key,
    w_value,
    w_out,
    norm_attn,
    norm_ffn,
    w_router,
    shared_gate,
    shared_up,
    shared_down,
    expert_gate,
    expert_up,
    expert_down,
    teacher,
    routes,
    cont_lengths,
    valid_mask,
):
    rows_dev, groups, model_width = hidden_in.shape
    token_local = rows_dev * groups
    head_count = lax.axis_size("head")
    cycle_count = lax.axis_size("blk")
    devices = head_count * cycle_count
    slices = devices // EXPERTS
    score_scale = HEAD_DIM ** (-0.5)
    flat_index = lax.axis_index("head") * cycle_count + lax.axis_index("blk")
    valid_total = lax.psum(jnp.sum(valid_mask.astype(jnp.float32)), ("head", "blk"))
    gathered = (
        lax.all_gather(w_query, ("head", "blk"), axis=0, tiled=True),
        lax.all_gather(w_key, ("head", "blk"), axis=0, tiled=True),
        lax.all_gather(w_value, ("head", "blk"), axis=0, tiled=True),
        lax.all_gather(w_out, ("head", "blk"), axis=0, tiled=True),
        lax.all_gather(w_router, ("head", "blk"), axis=0, tiled=True),
        lax.all_gather(shared_gate, ("head", "blk"), axis=0, tiled=True),
        lax.all_gather(shared_up, ("head", "blk"), axis=0, tiled=True),
        lax.all_gather(shared_down, ("head", "blk"), axis=0, tiled=True),
        lax.all_gather(norm_attn, ("head", "blk"), axis=0, tiled=True),
        lax.all_gather(norm_ffn, ("head", "blk"), axis=0, tiled=True),
    )
    (
        query_mat,
        key_mat,
        value_mat,
        out_mat,
        route_mat,
        share_gate,
        share_up,
        share_down,
        gain_low_attn,
        gain_low_ffn,
    ) = gathered
    gain_attn = gain_low_attn.astype(jnp.float32)
    gain_ffn = gain_low_ffn.astype(jnp.float32)
    local_pos = flat_index * rows_dev + jnp.arange(rows_dev, dtype=jnp.int32)
    local_begin = segment_starts(local_pos, cont_lengths)
    cosine_table, sine_table = rotary_tables(local_pos, local_begin)
    flat_in = hidden_in.reshape(token_local, model_width)
    normed_exact, scaling_attn = root_norm(flat_in, gain_attn)
    normed_attn = normed_exact.astype(jnp.bfloat16)
    head_shape = (rows_dev, groups, HEADS, HEAD_DIM)
    query_raw = jnp.dot(normed_attn, query_mat, preferred_element_type=jnp.float32).reshape(
        head_shape
    )
    key_raw = jnp.dot(normed_attn, key_mat, preferred_element_type=jnp.float32).reshape(head_shape)
    value_local = (
        jnp.dot(normed_attn, value_mat, preferred_element_type=jnp.float32)
        .astype(jnp.bfloat16)
        .reshape(head_shape)
    )
    query_local = rotate(query_raw, cosine_table, sine_table).astype(jnp.bfloat16)
    key_local = rotate(key_raw, cosine_table, sine_table).astype(jnp.bfloat16)
    regrouped = to_heads(jnp.stack([query_local, key_local, value_local], axis=0))
    queries = regrouped[0]
    key_rows = regrouped[1]
    value_rows = regrouped[2]
    query_count = queries.shape[0]
    query_pos = spread_position(
        lax.axis_index("blk") * query_count + jnp.arange(query_count, dtype=jnp.int32),
        rows_dev,
        head_count,
        cycle_count,
    )

    def key_place(global_row):
        return spread_position(global_row, rows_dev, head_count, cycle_count)

    query_begin = segment_starts(query_pos, cont_lengths)
    head_local = queries.shape[2]
    query_rows = queries.shape[0]
    start_state = (
        jnp.full((groups, head_local, query_rows), NEGATIVE, jnp.float32),
        jnp.zeros((groups, head_local, query_rows), jnp.float32),
        jnp.zeros((groups, head_local, query_rows, HEAD_DIM), jnp.float32),
    )
    stepper = forward_step(queries, query_pos, query_begin, key_place, score_scale)
    final_state = stepper(
        start_state,
        (
            lax.all_gather(key_rows, "blk", axis=0, tiled=True),
            lax.all_gather(value_rows, "blk", axis=0, tiled=True),
        ),
        jnp.int32(0),
    )
    row_top, row_total, weighted_sum = final_state
    heads_exact = (weighted_sum / row_total[..., None]).transpose(2, 0, 1, 3)
    log_total = row_top + jnp.log(row_total)
    heads_low = heads_exact.astype(jnp.bfloat16)
    attended = from_heads(heads_low[None])[0]
    attended_flat = attended.reshape(token_local, model_width)
    residual_mid = flat_in + jnp.dot(attended_flat, out_mat, preferred_element_type=jnp.float32)
    normed_mid, scaling_ffn = root_norm(residual_mid, gain_ffn)
    normed_ffn = normed_mid.astype(jnp.bfloat16)
    logits = jnp.dot(normed_ffn, route_mat, preferred_element_type=jnp.float32)
    route_flat = routes.reshape(token_local, TOP)
    route_onehot = (route_flat[:, :, None] == jnp.arange(EXPERTS, dtype=jnp.int32)).astype(
        jnp.float32
    )
    chosen = jnp.sum(route_onehot * logits[:, None, :], axis=-1)
    gate_probs = jax.nn.softmax(chosen, axis=1)
    shared_gate_in = jnp.dot(normed_ffn, share_gate, preferred_element_type=jnp.float32)
    shared_up_in = jnp.dot(normed_ffn, share_up, preferred_element_type=jnp.float32)
    shared_hidden = (apply_silu(shared_gate_in) * shared_up_in).astype(jnp.bfloat16)
    shared_out = jnp.dot(shared_hidden, share_down, preferred_element_type=jnp.float32)
    flat_routes = route_flat.reshape(-1)
    route_hits = (flat_routes[:, None] == jnp.arange(EXPERTS, dtype=jnp.int32)).astype(jnp.int32)
    ranking = jnp.sum((jnp.cumsum(route_hits, axis=0) - 1) * route_hits, axis=1)
    slot_of = (flat_routes * CAP + ranking).reshape(token_local, TOP)
    slot_ids = jnp.arange(EXPERTS * CAP, dtype=jnp.int32)
    place_first = (slot_ids[:, None] == slot_of[None, :, 0]).astype(jnp.bfloat16)
    place_second = (slot_ids[:, None] == slot_of[None, :, 1]).astype(jnp.bfloat16)
    sending = jnp.dot(
        place_first + place_second, normed_ffn, preferred_element_type=jnp.float32
    ).astype(jnp.bfloat16)
    gate_held, up_held, down_held = (expert_gate, expert_up, expert_down)
    outgoing = jnp.repeat(sending.reshape(EXPERTS, CAP, model_width), slices, axis=0)
    arrived = to_experts(outgoing).reshape(devices * CAP, model_width)
    inner_gate = jnp.dot(arrived, gate_held, preferred_element_type=jnp.float32)
    inner_up = jnp.dot(arrived, up_held, preferred_element_type=jnp.float32)
    inner_hidden = (apply_silu(inner_gate) * inner_up).astype(jnp.bfloat16)
    partial_out = jnp.dot(inner_hidden, down_held, preferred_element_type=jnp.float32)
    returned = from_experts(partial_out.reshape(devices, CAP, model_width))
    expert_rows = jnp.sum(returned.reshape(EXPERTS, slices, CAP, model_width), axis=1).reshape(
        EXPERTS * CAP, model_width
    )
    routed_first = jnp.take(expert_rows, slot_of[:, 0], axis=0)
    routed_second = jnp.take(expert_rows, slot_of[:, 1], axis=0)
    mixture = gate_probs[:, 0:1] * routed_first + gate_probs[:, 1:2] * routed_second
    layer_flat = residual_mid + shared_out + mixture
    keep_rows = valid_mask.reshape(token_local).astype(jnp.float32)[:, None]
    deviation = layer_flat - teacher.reshape(token_local, model_width)
    loss_local = jnp.sum(keep_rows * deviation * deviation)
    loss_total = lax.psum(loss_local, ("head", "blk"))
    loss_value = loss_total / (valid_total * model_width)
    grad_rows = keep_rows * deviation * (token_local * devices / valid_total)
    grad_gate = jnp.stack(
        [jnp.sum(grad_rows * routed_first, axis=-1), jnp.sum(grad_rows * routed_second, axis=-1)],
        axis=1,
    )
    grad_chosen = gate_probs * (grad_gate - jnp.sum(gate_probs * grad_gate, axis=1, keepdims=True))
    grad_logits = jnp.sum(route_onehot * grad_chosen[:, :, None], axis=1).astype(jnp.bfloat16)
    grad_route_mat = jnp.dot(normed_ffn.T, grad_logits, preferred_element_type=jnp.float32)
    grad_normed = jnp.dot(grad_logits, route_mat.T, preferred_element_type=jnp.float32)
    back_first = (gate_probs[:, 0:1] * grad_rows).astype(jnp.bfloat16)
    back_second = (gate_probs[:, 1:2] * grad_rows).astype(jnp.bfloat16)
    back_send = (
        jnp.dot(place_first, back_first, preferred_element_type=jnp.float32)
        + jnp.dot(place_second, back_second, preferred_element_type=jnp.float32)
    ).astype(jnp.bfloat16)
    back_arrived = to_experts(
        jnp.repeat(back_send.reshape(EXPERTS, CAP, model_width), slices, axis=0)
    ).reshape(devices * CAP, model_width)
    grad_inner = jnp.dot(back_arrived, down_held.T, preferred_element_type=jnp.float32)
    grad_down_held = jnp.dot(inner_hidden.T, back_arrived, preferred_element_type=jnp.float32)
    grad_inner_gate = (grad_inner * inner_up * silu_slope(inner_gate)).astype(jnp.bfloat16)
    grad_inner_up = (grad_inner * apply_silu(inner_gate)).astype(jnp.bfloat16)
    grad_gate_held = jnp.dot(arrived.T, grad_inner_gate, preferred_element_type=jnp.float32)
    grad_up_held = jnp.dot(arrived.T, grad_inner_up, preferred_element_type=jnp.float32)
    back_partial = jnp.dot(
        grad_inner_gate, gate_held.T, preferred_element_type=jnp.float32
    ) + jnp.dot(grad_inner_up, up_held.T, preferred_element_type=jnp.float32)
    grad_expert_gate, grad_expert_up, grad_expert_down = (
        grad_gate_held,
        grad_up_held,
        grad_down_held,
    )
    back_returned = from_experts(back_partial.reshape(devices, CAP, model_width))
    back_rows = jnp.sum(back_returned.reshape(EXPERTS, slices, CAP, model_width), axis=1).reshape(
        EXPERTS * CAP, model_width
    )
    grad_normed = (
        grad_normed
        + jnp.take(back_rows, slot_of[:, 0], axis=0)
        + jnp.take(back_rows, slot_of[:, 1], axis=0)
    )
    grad_shared_low = grad_rows.astype(jnp.bfloat16)
    grad_share_down = jnp.dot(shared_hidden.T, grad_shared_low, preferred_element_type=jnp.float32)
    grad_shared_hidden = jnp.dot(grad_shared_low, share_down.T, preferred_element_type=jnp.float32)
    grad_shared_gate_in = (grad_shared_hidden * shared_up_in * silu_slope(shared_gate_in)).astype(
        jnp.bfloat16
    )
    grad_shared_up_in = (grad_shared_hidden * apply_silu(shared_gate_in)).astype(jnp.bfloat16)
    grad_share_gate = jnp.dot(normed_ffn.T, grad_shared_gate_in, preferred_element_type=jnp.float32)
    grad_share_up = jnp.dot(normed_ffn.T, grad_shared_up_in, preferred_element_type=jnp.float32)
    grad_normed = (
        grad_normed
        + jnp.dot(grad_shared_gate_in, share_gate.T, preferred_element_type=jnp.float32)
        + jnp.dot(grad_shared_up_in, share_up.T, preferred_element_type=jnp.float32)
    )
    grad_mid_norm, grad_gain_ffn = root_norm_back(residual_mid, scaling_ffn, gain_ffn, grad_normed)
    grad_mid = grad_rows + grad_mid_norm
    grad_mid_low = grad_mid.astype(jnp.bfloat16)
    grad_out_mat = jnp.dot(attended_flat.T, grad_mid_low, preferred_element_type=jnp.float32)
    grad_attended = (
        jnp.dot(grad_mid_low, out_mat.T, preferred_element_type=jnp.float32)
        .astype(jnp.bfloat16)
        .reshape(head_shape)
    )
    grad_heads = to_heads(grad_attended[None])[0]
    offsets = jnp.sum(grad_heads.astype(jnp.float32) * heads_exact, axis=-1).transpose(1, 2, 0)
    row_stats = split_stats(log_total, offsets)
    back_stepper = backward_step(
        (queries, key_rows, value_rows, grad_heads, log_total, offsets),
        query_pos,
        query_begin,
        key_place,
        cont_lengths,
        score_scale,
    )
    zero_grad = jnp.zeros(queries.shape, jnp.float32)
    grad_state = back_stepper(
        (zero_grad, zero_grad, zero_grad),
        (
            lax.all_gather(queries, "blk", axis=0, tiled=True),
            lax.all_gather(key_rows, "blk", axis=0, tiled=True),
            lax.all_gather(value_rows, "blk", axis=0, tiled=True),
            lax.all_gather(grad_heads, "blk", axis=0, tiled=True),
            lax.all_gather(row_stats, "blk", axis=0, tiled=True),
        ),
        jnp.int32(0),
    )
    stacked_grads = jnp.stack([grad_state[0], grad_state[1], grad_state[2]], axis=0).astype(
        jnp.bfloat16
    )
    token_grads = from_heads(stacked_grads)
    grad_query_raw = (
        rotate_back(token_grads[0].astype(jnp.float32), cosine_table, sine_table)
        .astype(jnp.bfloat16)
        .reshape(token_local, model_width)
    )
    grad_key_raw = (
        rotate_back(token_grads[1].astype(jnp.float32), cosine_table, sine_table)
        .astype(jnp.bfloat16)
        .reshape(token_local, model_width)
    )
    grad_value_rows = token_grads[2].reshape(token_local, model_width)
    grad_query_mat = jnp.dot(normed_attn.T, grad_query_raw, preferred_element_type=jnp.float32)
    grad_key_mat = jnp.dot(normed_attn.T, grad_key_raw, preferred_element_type=jnp.float32)
    grad_value_mat = jnp.dot(normed_attn.T, grad_value_rows, preferred_element_type=jnp.float32)
    grad_normed_attn = (
        jnp.dot(grad_query_raw, query_mat.T, preferred_element_type=jnp.float32)
        + jnp.dot(grad_key_raw, key_mat.T, preferred_element_type=jnp.float32)
        + jnp.dot(grad_value_rows, value_mat.T, preferred_element_type=jnp.float32)
    )
    grad_in_norm, grad_gain_attn = root_norm_back(
        flat_in, scaling_attn, gain_attn, grad_normed_attn
    )
    input_grad = (grad_mid + grad_in_norm).reshape(rows_dev, groups, model_width)
    sharded = (
        lax.psum_scatter(grad_query_mat, ("head", "blk"), scatter_dimension=0, tiled=True),
        lax.psum_scatter(grad_key_mat, ("head", "blk"), scatter_dimension=0, tiled=True),
        lax.psum_scatter(grad_value_mat, ("head", "blk"), scatter_dimension=0, tiled=True),
        lax.psum_scatter(grad_out_mat, ("head", "blk"), scatter_dimension=0, tiled=True),
        lax.psum_scatter(grad_route_mat, ("head", "blk"), scatter_dimension=0, tiled=True),
        lax.psum_scatter(grad_share_gate, ("head", "blk"), scatter_dimension=0, tiled=True),
        lax.psum_scatter(grad_share_up, ("head", "blk"), scatter_dimension=0, tiled=True),
        lax.psum_scatter(grad_share_down, ("head", "blk"), scatter_dimension=0, tiled=True),
        lax.psum_scatter(grad_gain_attn, ("head", "blk"), scatter_dimension=0, tiled=True),
        lax.psum_scatter(grad_gain_ffn, ("head", "blk"), scatter_dimension=0, tiled=True),
    )
    return (
        layer_flat.reshape(rows_dev, groups, model_width),
        input_grad,
        loss_value,
        sharded[0],
        sharded[1],
        sharded[2],
        sharded[3],
        sharded[8],
        sharded[9],
        sharded[4],
        sharded[5],
        sharded[6],
        sharded[7],
        grad_expert_gate,
        grad_expert_up,
        grad_expert_down,
    )


def solution(mesh):
    placed = (
        P(("head", "blk"), None, None),
        P(("head", "blk"), None),
        P(("head", "blk"), None),
        P(("head", "blk"), None),
        P(("head", "blk"), None),
        P(("head", "blk")),
        P(("head", "blk")),
        P(("head", "blk"), None),
        P(("head", "blk"), None),
        P(("head", "blk"), None),
        P(("head", "blk"), None),
        P(None, ("head", "blk")),
        P(None, ("head", "blk")),
        P(("head", "blk"), None),
        P(("head", "blk"), None, None),
        P(("head", "blk"), None, None),
        P(),
        P(("head", "blk"), None),
    )
    return jax.shard_map(
        on_device,
        mesh=mesh,
        in_specs=placed,
        out_specs=(
            P(("head", "blk"), None, None),
            P(("head", "blk"), None, None),
            P(),
            P(("head", "blk"), None),
            P(("head", "blk"), None),
            P(("head", "blk"), None),
            P(("head", "blk"), None),
            P(("head", "blk")),
            P(("head", "blk")),
            P(("head", "blk"), None),
            P(("head", "blk"), None),
            P(("head", "blk"), None),
            P(("head", "blk"), None),
            P(None, ("head", "blk")),
            P(None, ("head", "blk")),
            P(("head", "blk"), None),
        ),
        check_vma=False,
    )
```

profile of v0, /device:TPU:0, one launch (start us, length us, event | category | flops | bytes accessed | tf_op | source)
XLA Modules:
  0.0 1805.9 jit_solution(1915026871886538857)
XLA Ops:
  11.2 42.1 %all-reduce.6 = (bf16[768]{0:T(1024)(128)(2,1)S(1)}, bf16[768]{0:T(1024)(128)(2,1)}) all-reduce(bf16[768]{0:T(1024)(128)(2,1)S(1)} %dynamic-update-slice, bf16[768]{0:T(1024)(128)(2,1)S(1)} %dynamic-update-slice.1), channel_id=1, replica_groups=mesh['head'=2,'blk'=16] {'head','blk'}, use_global_device_ids=true, to_apply=%add | all-reduce | flops 1536 | bytes 6144
  70.1 53.4 %all-gather.13.cloned.1.call-done = bf16[768,768]{1,0:T(8,128)(2,1)} async-done(((bf16[24,768]{1,0:T(8,128)(2,1)}), bf16[768,768]{1,0:T(8,128)(2,1)}) %all-gather.13.cloned.1.call-update) | async-done | bytes 1179664 | tf_op jit(solution)/shard_map/all_gather | solution.py:250
  130.4 49.0 %all-gather.17.cloned.1.call-done = bf16[768,768]{1,0:T(8,128)(2,1)} async-done(((bf16[24,768]{1,0:T(8,128)(2,1)}), bf16[768,768]{1,0:T(8,128)(2,1)}) %all-gather.17.cloned.1.call-update) | async-done | bytes 1179664 | tf_op jit(solution)/shard_map/all_gather | solution.py:252
  229.8 41.1 %all-gather.19.cloned.1.call-done = bf16[8192,1,6,64]{0,3,2,1:T(8,128)(2,1)} async-done(((bf16[512,1,6,64]{0,3,2,1:T(8,128)(2,1)}), bf16[8192,1,6,64]{0,3,2,1:T(8,128)(2,1)}) %all-gather.19.cloned.1.call-update) | async-done | bytes 6291472 | tf_op jit(solution)/shard_map/all_gather | solution.py:320
  270.9 40.7 %select_reduce_fusion = (f32[6,512]{1,0:T(8,128)S(1)}, f32[6,512,8192]{2,1,0:T(8,128)}) fusion(pred[512,8192]{1,0:T(8,128)(4,1)} %or_and_fusion.1, bf16[512,6,64]{0,2,1:T(8,128)(2,1)} %reshape.1766, bf16[8192,1,6,64]{0,3,2,1:T(8,128)(2,1)} %all-gather.19.cloned.1.call-done), kind=kOutput, calls=%fused_computation.8 | convolution fusion | flops 3296719872 | bytes 111554560 | tf_op jit(solution)/shard_map/qghd,kghd->ghqk/dot_general | solution.py:111
  312.3 36.1 %fusion.1 = f32[6,512]{1,0:T(8,128)S(1)} fusion(f32[6,512,8192]{2,1,0:T(8,128)} %get-tuple-element.166, f32[6,512]{1,0:T(8,128)S(1)} %broadcast_maximum_fusion, pred[512,8192]{1,0:T(8,128)(4,1)} %or_and_fusion.1), kind=kLoop, calls=%fused_computation.10 | loop fusion | flops 125826048 | bytes 104882176 | tf_op jit(solution)/shard_map/reduce_sum | solution.py:117
  348.4 40.7 %fusion.80 = f32[512,1,6,64]{0,3,2,1:T(8,128)S(1)} fusion(bf16[8192,1,6,64]{0,3,2,1:T(8,128)(2,1)} %all-gather.21.cloned.1.call-done, f32[6,512,8192]{2,1,0:T(8,128)} %get-tuple-element.166, f32[6,512]{1,0:T(8,128)S(1)} %broadcast_maximum_fusion, pred[512,8192]{1,0:T(8,128)(4,1)} %or_and_fusion.1, f32[6,512]{1,0:T(8,128)S(1)} %fusion.1), kind=kOutput, calls=%fused_computation.77 | convolution fusion | flops 3347251200 | bytes 111960064 | tf_op jit(solution)/shard_map/ghqk,kghd->ghqd/dot_general | solution.py:118
  420.2 87.4 %all-to-all-done.2 = bf16[32,64,768]{2,1,0:T(8,128)(2,1)} async-done(((bf16[32,64,768]{2,1,0:T(8,128)(2,1)}), bf16[32,64,768]{2,1,0:T(8,128)(2,1)}, u32[]{:S(2)}, u32[]{:S(2)}) %all-to-all-start.2) | async-done | bytes 3145760 | tf_op jit(solution)/shard_map/all_to_all | solution.py:211
  534.7 104.8 %psum.14 = f32[]{:T(128)} all-reduce(f32[]{:T(128)} %convert_reduce_fusion.2), channel_id=1, replica_groups=mesh['head'=2,'blk'=16] {'head','blk'}, use_global_device_ids=true, to_apply=%region_15.17 | all-reduce | flops 1 | bytes 8 | tf_op jit(solution)/shard_map/psum | solution.py:248
  640.0 41.2 %all-gather = bf16[32,24,16]{1,2,0:T(8,128)(2,1)S(1)} all-gather(bf16[1,24,16]{1,2,0:T(8,128)(2,1)S(1)} %bitcast.400), channel_id=1, replica_groups=mesh['head'=2,'blk'=16] {'head','blk'}, dimensions={0}, use_global_device_ids=true | all-gather | bytes 25344 | tf_op jit(solution)/shard_map/all_gather | solution.py:254
  720.3 108.6 %all-to-all-done.4 = bf16[32,64,768]{2,1,0:T(8,128)(2,1)} async-done(((bf16[32,64,768]{2,1,0:T(8,128)(2,1)}), bf16[32,64,768]{2,1,0:T(8,128)(2,1)}, u32[]{:S(2)}, u32[]{:S(2)}) %all-to-all-start.4) | async-done | bytes 3145760 | tf_op jit(solution)/shard_map/all_to_all | solution.py:211
  862.2 62.5 %all-to-all-done.5 = bf16[32,64,768]{2,1,0:T(8,128)(2,1)} async-done(((bf16[32,64,768]{2,1,0:T(8,128)(2,1)}), bf16[32,64,768]{2,1,0:T(8,128)(2,1)}, u32[]{:S(2)}, u32[]{:S(2)}) %all-to-all-start.5) | async-done | bytes 3145760 | tf_op jit(solution)/shard_map/all_to_all | solution.py:215
  972.0 38.5 %fusion.22 = f32[6,8192,512]{2,1,0:T(8,128)} fusion(bf16[512,6,64]{0,2,1:T(8,128)(2,1)S(1)} %reshape.1786, bf16[8192,1,6,64]{0,3,2,1:T(8,128)(2,1)} %all-gather.31.cloned.1.call-done), kind=kOutput, calls=%fused_computation.34 | convolution fusion | flops 3221225472 | bytes 107347968 | tf_op jit(solution)/shard_map/pghd,kghd->ghpk/dot_general | solution.py:174
  1013.0 19.0 %all_gather.60 = bf16[8192,4,1,6]{0,3,2,1:T(8,128)(2,1)S(1)} all-gather(bf16[512,4,1,6]{0,3,2,1:T(8,128)(2,1)S(1)} %pad_maximum_fusion.2), channel_id=1, replica_groups=mesh['head'=2,'blk'=16] {'blk'}, dimensions={0}, use_global_device_ids=true | all-gather | bytes 417792 | tf_op jit(solution)/shard_map/all_gather | solution.py:458
  1032.1 57.5 %fusion.70 = bf16[1,512,1,6,64]{1,4,3,2,0:T(8,128)(2,1)} fusion(f32[6,512,8192]{2,1,0:T(8,128)} %get-tuple-element.166, f32[6,512]{1,0:T(8,128)S(1)} %bitcast.390, f32[6,512]{1,0:T(8,128)S(1)} %get-tuple-element.128, pred[512,8192]{1,0:T(8,128)(4,1)} %or_and_fusion.1, bf16[512,6,64]{0,2,1:T(8,128)(2,1)S(1)} %reshape.1784, ...), kind=kOutput, calls=%fused_computation.73 | convolution fusion | flops 6593839104 | bytes 118251520 | tf_op jit(solution)/shard_map/ghqk,kghd->qghd/dot_general | solution.py:157
  1089.7 46.1 %fusion.55 = bf16[1,512,1,6,64]{1,4,3,2,0:T(8,128)(2,1)S(1)} fusion(f32[6,8192,512]{2,1,0:T(8,128)} %fusion.22, f32[6,8192]{1,0:T(8,128)S(1)} %get-tuple-element.151, f32[6,8192]{1,0:T(8,128)S(1)} %get-tuple-element.152, pred[8192,512]{1,0:T(8,128)(4,1)} %or_and_fusion, bf16[512,6,64]{0,2,1:T(8,128)(2,1)S(1)} %copy-done.42, ...), kind=kOutput, calls=%fused_computation.70 | convolution fusion | flops 6593839104 | bytes 118620160 | tf_op jit(solution)/shard_map/ghpk,pghd->kghd/dot_general | solution.py:183
  1135.8 38.4 %fusion.40 = bf16[1,512,1,6,64]{1,4,3,2,0:T(8,128)(2,1)S(1)} fusion(f32[6,8192,512]{2,1,0:T(8,128)} %fusion.22, f32[6,8192]{1,0:T(8,128)S(1)} %get-tuple-element.152, pred[8192,512]{1,0:T(8,128)(4,1)} %or_and_fusion, bf16[8192,1,6,64]{0,3,2,1:T(8,128)(2,1)} %all-gather.33.cloned.1.call-done), kind=kOutput, calls=%fused_computation.64 | convolution fusion | flops 3322085376 | bytes 111738880 | tf_op jit(solution)/shard_map/ghpk,pghd->kghd/dot_general | solution.py:191
  1182.6 28.9 %all_to_all.82 = bf16[2,2,147456]{2,1,0:T(2,128)(2,1)} all-to-all(bf16[2,2,147456]{2,1,0:T(2,128)(2,1)} %reshape.1855), channel_id=1, replica_groups=mesh['head'=2,'blk'=16] {'head'}, dimensions={0} | all-to-all | bytes 2359296 | tf_op jit(solution)/shard_map/all_to_all | solution.py:207
  1256.1 39.5 %all-reduce.5 = (f32[]{:T(128)}, f32[768]{0:T(1024)S(1)}, f32[768]{0:T(1024)S(1)}, f32[768,16]{0,1:T(8,128)S(1)}) all-reduce(f32[]{:T(128)} %get-tuple-element.136, f32[768]{0:T(1024)S(1)} %get-tuple-element.115, f32[768]{0:T(1024)S(1)} %copy-done.65, f32[768,16]{0,1:T(8,128)} %fusion.193), channel_id=1, replica_groups=mesh['head'=2,'blk'=16] {'head','blk'}, use_global_device_ids=true, to_apply=%region_26.28 | all-reduce | flops 13825 | bytes 110600 | tf_op jit(solution)/shard_map/psum | solution.py:373
  1301.9 78.9 %reduce-scatter.19.cloned.1.call-done = f32[24,2048]{1,0:T(8,128)} async-done(((f32[768,2048]{1,0:T(8,128)}), f32[24,2048]{1,0:T(8,128)}) %reduce-scatter.19.cloned.1.call-update) | async-done | bytes 196624 | tf_op jit(solution)/shard_map/reduce_scatter | solution.py:496
  1380.8 104.8 %reduce-scatter.15.cloned.1.call-done = f32[24,768]{1,0:T(8,128)} async-done(((f32[768,768]{1,0:T(8,128)}), f32[24,768]{1,0:T(8,128)}) %reduce-scatter.15.cloned.1.call-update) | async-done | bytes 73744 | tf_op jit(solution)/shard_map/reduce_scatter | solution.py:493
  1485.6 103.8 %reduce-scatter.11.cloned.1.call-done = f32[24,768]{1,0:T(8,128)} async-done(((f32[768,768]{1,0:T(8,128)}), f32[24,768]{1,0:T(8,128)}) %reduce-scatter.11.cloned.1.call-update) | async-done | bytes 73744 | tf_op jit(solution)/shard_map/reduce_scatter | solution.py:491
  1589.3 104.7 %reduce-scatter.9.cloned.1.call-done = f32[24,768]{1,0:T(8,128)} async-done(((f32[768,768]{1,0:T(8,128)}), f32[24,768]{1,0:T(8,128)}) %reduce-scatter.9.cloned.1.call-update) | async-done | bytes 73744 | tf_op jit(solution)/shard_map/reduce_scatter | solution.py:490
  1694.0 103.8 %reduce-scatter.13.cloned.1.call-done = f32[24,768]{1,0:T(8,128)} async-done(((f32[768,768]{1,0:T(8,128)}), f32[24,768]{1,0:T(8,128)}) %reduce-scatter.13.cloned.1.call-update) | async-done | bytes 73744 | tf_op jit(solution)/shard_map/reduce_scatter | solution.py:492
  (392 shorter events, 315.6 us)
Async XLA Ops:
  7.2 60.5 %all-gather.15.cloned.1.call-start = ((), (), s32[]{:S(2)}) async-start(), calls=%async_computation.16 | async-start | bytes 1216512 | tf_op jit(solution)/shard_map/all_gather | solution.py:251
  7.9 115.6 %all-gather.13.cloned.1.call-start = ((), (), s32[]{:S(2)}) async-start(), calls=%async_computation.15 | async-start | bytes 1216512 | tf_op jit(solution)/shard_map/all_gather | solution.py:250
  8.7 170.7 %all-gather.17.cloned.1.call-start = ((), (), s32[]{:S(2)}) async-start(), calls=%async_computation.17 | async-start | bytes 1216512 | tf_op jit(solution)/shard_map/all_gather | solution.py:252
  9.4 261.5 %all-gather.19.cloned.1.call-start = ((), (), s32[]{:S(2)}) async-start(), calls=%async_computation.18 | async-start | bytes 6684672 | tf_op jit(solution)/shard_map/all_gather | solution.py:320
  206.2 142.2 %all-gather.21.cloned.1.call-start = ((), (), s32[]{:S(2)}) async-start(), calls=%async_computation.19 | async-start | bytes 6684672 | tf_op jit(solution)/shard_map/all_gather | solution.py:321
  207.3 203.1 %all-gather.23.cloned.1.call-start = ((), (), s32[]{:S(2)}) async-start(), calls=%async_computation.20 | async-start | bytes 1216512 | tf_op jit(solution)/shard_map/all_gather | solution.py:253
  207.8 475.9 %all-gather.25.cloned.1.call-start = ((), (), s32[]{:S(2)}) async-start(), calls=%async_computation.21 | async-start | bytes 3244032 | tf_op jit(solution)/shard_map/all_gather | solution.py:255
  394.2 12.2 all-to-all-start.1
  415.9 91.7 %all-to-all-start.2 = ((bf16[32,64,768]{2,1,0:T(8,128)(2,1)}), bf16[32,64,768]{2,1,0:T(8,128)(2,1)}, u32[]{:S(2)}, u32[]{:S(2)}) async-start(bf16[32,64,768]{2,1,0:T(8,128)(2,1)} %bitcast.358), calls=%async_computation.2 | async-start | bytes 6291456 | tf_op jit(solution)/shard_map/all_to_all | solution.py:211
  419.4 268.5 %all-gather.27.cloned.1.call-start = ((), (), s32[]{:S(2)}) async-start(), calls=%async_computation.22 | async-start | bytes 3244032 | tf_op jit(solution)/shard_map/all_gather | solution.py:256
  529.6 163.7 %all-to-all-start.3 = ((bf16[32,64,768]{2,1,0:T(8,128)(2,1)}), bf16[32,64,768]{2,1,0:T(8,128)(2,1)}, u32[]{:S(2)}, u32[]{:S(2)}) async-start(bf16[32,64,768]{2,1,0:T(8,128)(2,1)} %bitcast.380), calls=%async_computation.3 | async-start | bytes 6291456 | tf_op jit(solution)/shard_map/all_to_all | solution.py:215
  533.3 172.7 %all-gather.29.cloned.1.call-start = ((), (), s32[]{:S(2)}) async-start(), calls=%async_computation.23 | async-start | bytes 3244032 | tf_op jit(solution)/shard_map/all_gather | solution.py:257
  715.1 113.7 %all-to-all-start.4 = ((bf16[32,64,768]{2,1,0:T(8,128)(2,1)}), bf16[32,64,768]{2,1,0:T(8,128)(2,1)}, u32[]{:S(2)}, u32[]{:S(2)}) async-start(bf16[32,64,768]{2,1,0:T(8,128)(2,1)} %bitcast.357), calls=%async_computation.4 | async-start | bytes 6291456 | tf_op jit(solution)/shard_map/all_to_all | solution.py:211
  718.8 253.3 %all-gather.31.cloned.1.call-start = ((), (), s32[]{:S(2)}) async-start(), calls=%async_computation.24 | async-start | bytes 6684672 | tf_op jit(solution)/shard_map/all_gather | solution.py:454
  848.7 76.1 %all-to-all-start.5 = ((bf16[32,64,768]{2,1,0:T(8,128)(2,1)}), bf16[32,64,768]{2,1,0:T(8,128)(2,1)}, u32[]{:S(2)}, u32[]{:S(2)}) async-start(bf16[32,64,768]{2,1,0:T(8,128)(2,1)} %bitcast.381), calls=%async_computation.5 | async-start | bytes 6291456 | tf_op jit(solution)/shard_map/all_to_all | solution.py:215
  852.3 237.4 %all-gather.33.cloned.1.call-start = ((), (), s32[]{:S(2)}) async-start(), calls=%async_computation.25 | async-start | bytes 6684672 | tf_op jit(solution)/shard_map/all_gather | solution.py:457
  948.6 353.3 %reduce-scatter.21.cloned.1.call-start = ((), (), s32[]{:S(2)}) async-start(), calls=%async_computation.32 | async-start | bytes 6488064 | tf_op jit(solution)/shard_map/reduce_scatter | solution.py:497
  952.5 349.4 %reduce-scatter.17.cloned.1.call-start = ((), (), s32[]{:S(2)}) async-start(), calls=%async_computation.30 | async-start | bytes 6488064 | tf_op jit(solution)/shard_map/reduce_scatter | solution.py:495
  957.4 423.4 %reduce-scatter.19.cloned.1.call-start = ((), (), s32[]{:S(2)}) async-start(), calls=%async_computation.31 | async-start | bytes 6488064 | tf_op jit(solution)/shard_map/reduce_scatter | solution.py:496
  962.3 523.2 %reduce-scatter.15.cloned.1.call-start = ((), (), s32[]{:S(2)}) async-start(), calls=%async_computation.29 | async-start | bytes 2433024 | tf_op jit(solution)/shard_map/reduce_scatter | solution.py:493
  1012.5 576.8 %reduce-scatter.11.cloned.1.call-start = ((), (), s32[]{:S(2)}) async-start(), calls=%async_computation.27 | async-start | bytes 2433024 | tf_op jit(solution)/shard_map/reduce_scatter | solution.py:491
  1221.1 472.9 %reduce-scatter.9.cloned.1.call-start = ((), (), s32[]{:S(2)}) async-start(), calls=%async_computation.26 | async-start | bytes 2433024 | tf_op jit(solution)/shard_map/reduce_scatter | solution.py:490
  1223.2 574.5 %reduce-scatter.13.cloned.1.call-start = ((), (), s32[]{:S(2)}) async-start(), calls=%async_computation.28 | async-start | bytes 2433024 | tf_op jit(solution)/shard_map/reduce_scatter | solution.py:492
  1253.2 544.6 %copy-start.1 = (bf16[1024,768]{1,0:T(8,128)(2,1)S(1)}, bf16[1024,768]{1,0:T(8,128)(2,1)}, u32[]{:S(2)}) copy-start(bf16[1024,768]{1,0:T(8,128)(2,1)} %param.33) | copy-start | bytes 4718596
  (92 other events, 3771.5 us)
Sparse Core Ops, SparseCore 0:
  10.9 56.7 all-gather.14
  70.6 52.8 all-gather.12
  126.4 52.9 all-gather.16
  206.3 64.5 all-gather.18
  273.5 63.8 all-gather.20
  340.1 52.1 all-gather.22
  395.2 75.2 all-gather.24
  473.4 61.5 all-gather.26
  537.8 76.9 all-gather.28
  721.5 103.0 all-gather.30
  948.7 61.8 all-gather.32
  1016.6 112.4 reduce-scatter.20
  1136.3 124.8 reduce-scatter.16
  1267.2 113.4 reduce-scatter.18
  1387.3 98.1 reduce-scatter.14
  1491.3 97.9 reduce-scatter.10
  1595.9 98.0 reduce-scatter.8
  1699.7 97.9 reduce-scatter.12
where the time goes:
time: 1810 us
  waiting for transfers between devices  918 us (51%)
  matrix products  389 us (21%)
  blocking collectives  304 us (17%)
  other arithmetic  81.5 us (5%)
  local copies, waits for them, and re-layouts  74.3 us (4%)
  starting transfers between devices  20.3 us (1%)
  between operations  19 us (1%)
    all_to_all x2, waiting for transfers between devices, to_experts(): lax.all_to_all(buffer_rows, ('head', 'blk'), split_axis=0, concat_axis=0,...  196 us
    reduce_scatter x1, waiting for transfers between devices, on_device(): lax.psum_scatter(grad_out_mat, ('head', 'blk'), scatter_dimension=0, tile...  105 us
    psum x1, blocking collectives, on_device(): lax.psum(jnp.sum(valid_mask.astype(jnp.float32)), ('head', 'blk'))  105 us
    reduce_scatter x1, waiting for transfers between devices, on_device(): lax.psum_scatter(grad_query_mat, ('head', 'blk'), scatter_dimension=0, ti...  105 us
    reduce_scatter x1, waiting for transfers between devices, on_device(): lax.psum_scatter(grad_value_mat, ('head', 'blk'), scatter_dimension=0, ti...  104 us
    reduce_scatter x1, waiting for transfers between devices, on_device(): lax.psum_scatter(grad_key_mat, ('head', 'blk'), scatter_dimension=0, tile...  104 us
    reduce_scatter x1, waiting for transfers between devices, on_device(): lax.psum_scatter(grad_share_up, ('head', 'blk'), scatter_dimension=0, til...  78.9 us
    all_to_all x2, waiting for transfers between devices, from_experts(): lax.all_to_all(buffer_rows.astype(jnp.bfloat16), ('head', 'blk'), split_a...  62.5 us
  transfers between devices with their start and end apart: 23, of which 13 were waited for; matrix products, arithmetic and copies ran while one was open for 29% of the time, Pallas kernels for 0%

commit v1 on v0

v1 whole, which is shorter than its diff:
```python
import functools
import math

import jax
import jax.numpy as jnp
from jax import lax
from jax.experimental import pallas as pl
from jax.experimental.pallas import tpu as pltpu
from jax.sharding import PartitionSpec as P

HEADS = 12
HEAD_DIM = 64
EXPERTS = 16
TOP = 2
PROMPT = 4096
LONGEST = 768
CAP = 64

EPSILON = 1e-06
NEGATIVE = -1e30
SCORE_SCALE = HEAD_DIM ** (-0.5)
EXP_SCALE = SCORE_SCALE * math.log2(math.e)

TILE = 256
FWD_WIDE, FWD_MASK = 8, 4
BWD_WIDE, BWD_MASK = 4, 2

MESH_ID = pl.DeviceIdType.MESH
AXES = ("head", "blk")


def apply_silu(argument):
    return argument * jax.nn.sigmoid(argument)


def silu_slope(argument):
    sigmoid_val = jax.nn.sigmoid(argument)
    return sigmoid_val * (1.0 + argument * (1.0 - sigmoid_val))


def root_norm(inputs, gain_vec):
    scaling = lax.rsqrt(jnp.mean(inputs * inputs, axis=-1, keepdims=True) + EPSILON)
    return (inputs * scaling * gain_vec, scaling)


def root_norm_back(inputs, scaling, gain_vec, upstream):
    weighted = gain_vec * upstream
    through = scaling * weighted - inputs * scaling**3 * jnp.mean(
        weighted * inputs, axis=-1, keepdims=True
    )
    return (through, jnp.sum(upstream * inputs * scaling, axis=0))


def segment_starts(positions, cont_lengths):
    run_ends = jnp.cumsum(cont_lengths, axis=1)
    begins = PROMPT + run_ends - cont_lengths
    passed = begins[None, :, :] <= positions[:, None, None]
    return jnp.max(jnp.where(passed, begins[None], 0), axis=-1)


def rotary_tables(positions, run_begin):
    relative = jnp.where(
        positions[:, None] < PROMPT, positions[:, None], PROMPT + positions[:, None] - run_begin
    )
    angle_pos = relative.astype(jnp.float32).reshape(1, -1)
    half_dim = HEAD_DIM // 2
    frequency = jnp.exp(
        jnp.arange(half_dim, dtype=jnp.int32).astype(jnp.float32)
        * (-2.0 * math.log(10000.0) / HEAD_DIM)
    )
    angles = angle_pos * frequency[:, None]
    return (jnp.cos(angles), jnp.sin(angles))


def flat_index(cols):
    return lax.axis_index("head") * cols + lax.axis_index("blk")


def coords(flat, cols):
    return (lax.div(flat, cols), lax.rem(flat, cols))


def greet(flat, cols):
    pl.semaphore_signal(
        pltpu.get_barrier_semaphore(),
        inc=1,
        device_id=coords(flat, cols),
        device_id_type=MESH_ID,
    )


def remote(source, target, send_sem, recv_sem, flat, cols):
    return pltpu.make_async_remote_copy(
        src_ref=source,
        dst_ref=target,
        send_sem=send_sem,
        recv_sem=recv_sem,
        device_id=coords(flat, cols),
        device_id_type=MESH_ID,
    )


def loop(first, last, body):
    def step(index, carry):
        body(index)
        return carry

    lax.fori_loop(first, last, step, 0)


def greet_partners(cols, size, partners):
    me = flat_index(cols)
    mine, group = lax.rem(me, size), lax.div(me, size)
    loop(1, partners, lambda s: greet(lax.rem(group + s, partners) * size + mine, cols))
    for t in range(1, size):
        greet(group * size + lax.rem(mine + t, size), cols)
    pl.semaphore_wait(pltpu.get_barrier_semaphore(), partners + size - 2)
    return mine, group


class Work:
    def __init__(self, arrays, out_shape, body, reuse=None):
        self.arrays, self.out_shape, self.body = list(arrays), list(out_shape), body
        self.reuse = reuse or {}

    def own_buffers(self):
        return [i for i in range(len(self.out_shape)) if i not in self.reuse]

    def scratch(self):
        held = self.arrays + [self.out_shape[i] for i in self.own_buffers()]
        total = len(self.arrays) + len(self.out_shape)
        return [pltpu.VMEM(a.shape, a.dtype) for a in held] + [pltpu.SemaphoreType.DMA((total,))]

    def bind(self, refs):
        count, total = len(self.arrays), len(self.arrays) + len(self.out_shape)
        inputs, outputs = refs[:count], refs[count:total]
        held_in, rest, sems = refs[total : total + count], refs[total + count : -1], refs[-1]
        held_out = [None] * len(outputs)
        for buffer, i in zip(rest, self.own_buffers()):
            held_out[i] = buffer
        for i, source in self.reuse.items():
            held_out[i] = held_in[source]
        loads = [
            pltpu.make_async_copy(inputs[i], held_in[i], sems.at[i]) for i in range(count)
        ]
        stores = [
            pltpu.make_async_copy(held_out[i], outputs[i], sems.at[count + i])
            for i in range(len(outputs))
        ]

        def begin():
            for copy in loads:
                copy.start()

        def run():
            for copy in loads:
                copy.wait()
            self.body(held_in, held_out, [copy.start for copy in stores])

        def end():
            for copy in stores:
                copy.wait()

        return begin, run, end


def split_refs(refs, count, work):
    extra_in = len(work.arrays) if work else 0
    extra_out = len(work.out_shape) if work else 0
    inputs, refs = refs[:count], refs[count:]
    work_in, refs = refs[:extra_in], refs[extra_in:]
    outputs, refs = refs[:count], refs[count:]
    work_out, refs = refs[:extra_out], refs[extra_out:]
    if not work:
        return inputs, outputs, refs, (lambda: None,) * 3
    held = extra_in + len(work.own_buffers()) + 1
    return inputs, outputs, refs[:-held], work.bind(work_in + work_out + refs[-held:])


def spread_kernel(cols, size, partners, work, count, *refs):
    inputs, outputs, sems, (begin, run, end) = split_refs(refs, count, work)
    begin()
    mine, group = greet_partners(cols, size, partners)

    def far(i, s):
        send, recv = sems[5 * i], sems[5 * i + 1]
        other = lax.rem(group + s, partners)
        return remote(
            inputs[i].at[other], outputs[i].at[mine, group], send.at[s], recv.at[s], other * size + mine, cols
        )

    def near(i, s, t):
        send, recv = sems[5 * i + 2], sems[5 * i + 3]
        block = outputs[i].at[mine, lax.rem(group - s + partners, partners)]
        target = group * size + lax.rem(mine + t, size)
        return remote(block, block, send.at[s, t], recv.at[s, t], target, cols)

    def own(i):
        return pltpu.make_async_copy(inputs[i].at[group], outputs[i].at[mine, group], sems[5 * i + 4])

    def each(action):
        for i in range(count):
            action(i)

    def near_all(s, action):
        for i in range(count):
            for t in range(1, size):
                action(near(i, s, t))

    each(lambda i: own(i).start())
    loop(1, partners, lambda s: each(lambda i: far(i, s).start()))
    each(lambda i: own(i).wait())
    near_all(0, lambda copy: copy.start())
    run()

    def relay(s):
        each(lambda i: far(i, s).wait_recv())
        near_all(s, lambda copy: copy.start())

    loop(1, partners, relay)
    loop(1, partners, lambda s: each(lambda i: far(i, s).wait_send()))
    loop(0, partners, lambda s: near_all(s, lambda copy: copy.wait()))
    end()


def spread(arrays, cols, size, partners, collective_id, work=None):
    count = len(arrays)
    out_shape, scratch = [], []
    for array in arrays:
        block = array.shape[1:]
        out_shape.append(jax.ShapeDtypeStruct((size, partners) + block, array.dtype))
        scratch += [
            pltpu.SemaphoreType.DMA((partners,)),
            pltpu.SemaphoreType.DMA((partners,)),
            pltpu.SemaphoreType.DMA((partners, size)),
            pltpu.SemaphoreType.DMA((partners, size)),
            pltpu.SemaphoreType.DMA,
        ]
    extra = []
    if work:
        extra, out_shape, scratch = work.arrays, out_shape + work.out_shape, scratch + work.scratch()
    return pl.pallas_call(
        functools.partial(spread_kernel, cols, size, partners, work, count),
        out_shape=out_shape,
        in_specs=[pl.BlockSpec(memory_space=pl.ANY)] * (count + len(extra)),
        out_specs=[pl.BlockSpec(memory_space=pl.ANY)] * len(out_shape),
        scratch_shapes=scratch,
        compiler_params=pltpu.CompilerParams(
            collective_id=collective_id, has_side_effects=True, vmem_limit_bytes=52 * 2**20
        ),
    )(*arrays, *extra)


def collect_kernel(cols, size, partners, work, count, *refs):
    inputs, outputs, scratch, (begin, run, end) = split_refs(refs, count, work)
    begin()
    mine, group = greet_partners(cols, size, partners)

    def near(i, s, t):
        inbox, send, recv = scratch[7 * i + 1], scratch[7 * i + 2], scratch[7 * i + 3]
        other = lax.rem(group + s, partners)
        member = lax.rem(mine + t, size)
        return remote(
            inputs[i].at[member, other],
            inbox.at[t - 1, other],
            send.at[s, t],
            recv.at[s, t],
            group * size + member,
            cols,
        )

    def far(i, s):
        stage, send, recv = scratch[7 * i], scratch[7 * i + 4], scratch[7 * i + 5]
        other = lax.rem(group + s, partners)
        return remote(
            stage.at[other], outputs[i].at[group], send.at[s], recv.at[s], other * size + mine, cols
        )

    def own(i):
        return pltpu.make_async_copy(
            scratch[7 * i].at[group], outputs[i].at[group], scratch[7 * i + 6]
        )

    def each(action):
        for i in range(count):
            action(i)

    def near_all(s, action):
        for i in range(count):
            for t in range(1, size):
                action(near(i, s, t))

    def add(s):
        other = lax.rem(group + s, partners)
        for i in range(count):
            stage, inbox = scratch[7 * i], scratch[7 * i + 1]
            total = inputs[i][mine, other].astype(jnp.float32)
            for t in range(1, size):
                total = total + inbox[t - 1, other].astype(jnp.float32)
            stage[other] = total.astype(stage.dtype)

    loop(1, partners, lambda s: near_all(s, lambda copy: copy.start()))
    near_all(0, lambda copy: copy.start())

    def relay(s):
        near_all(s, lambda copy: copy.wait_recv())
        add(s)
        each(lambda i: far(i, s).start())

    loop(1, partners, relay)
    near_all(0, lambda copy: copy.wait_recv())
    add(0)
    each(lambda i: own(i).start())
    run()
    loop(0, partners, lambda s: near_all(s, lambda copy: copy.wait_send()))
    loop(1, partners, lambda s: each(lambda i: far(i, s).wait()))
    each(lambda i: own(i).wait())
    end()


def collect(arrays, cols, collective_id, work=None):
    count = len(arrays)
    size, partners = arrays[0].shape[:2]
    out_shape, scratch = [], []
    for array in arrays:
        block = array.shape[2:]
        out_shape.append(jax.ShapeDtypeStruct((partners,) + block, array.dtype))
        scratch += [
            pltpu.VMEM((partners,) + block, array.dtype),
            pltpu.VMEM((size - 1, partners) + block, array.dtype),
            pltpu.SemaphoreType.DMA((partners, size)),
            pltpu.SemaphoreType.DMA((partners, size)),
            pltpu.SemaphoreType.DMA((partners,)),
            pltpu.SemaphoreType.DMA((partners,)),
            pltpu.SemaphoreType.DMA,
        ]
    extra = []
    if work:
        extra, out_shape, scratch = work.arrays, out_shape + work.out_shape, scratch + work.scratch()
    return pl.pallas_call(
        functools.partial(collect_kernel, cols, size, partners, work, count),
        out_shape=out_shape,
        in_specs=[pl.BlockSpec(memory_space=pltpu.VMEM)] * count
        + [pl.BlockSpec(memory_space=pl.ANY)] * len(extra),
        out_specs=[pl.BlockSpec(memory_space=pl.ANY)] * len(out_shape),
        scratch_shapes=scratch,
        compiler_params=pltpu.CompilerParams(
            collective_id=collective_id, has_side_effects=True, vmem_limit_bytes=52 * 2**20
        ),
    )(*arrays, *extra)


def spot():
    column = lax.axis_index("blk")
    return (
        lax.axis_index("head"),
        lax.div(column, 4),
        lax.rem(lax.div(column, 2), 2),
        lax.rem(column, 2),
    )


def at_spot(head, depth, x, core):
    return (head, depth * 4 + x * 2 + core)


def push(source, target, send_sem, recv_sem, device):
    return pltpu.make_async_remote_copy(
        src_ref=source,
        dst_ref=target,
        send_sem=send_sem,
        recv_sem=recv_sem,
        device_id=device,
        device_id_type=MESH_ID,
    )


def greet_mesh(depths):
    head, depth, x, core = spot()
    barrier = pltpu.get_barrier_semaphore()

    def signal(device):
        pl.semaphore_signal(barrier, inc=1, device_id=device, device_id_type=MESH_ID)

    loop(1, depths, lambda s: signal(at_spot(head, lax.rem(depth + s, depths), x, core)))
    signal(at_spot(head, depth, 1 - x, core))
    signal(at_spot(1 - head, depth, x, core))
    signal(at_spot(head, depth, x, 1 - core))
    pl.semaphore_wait(barrier, depths + 2)


GATHER_SEMS = 13


def gather_sems(depths):
    row, square = pltpu.SemaphoreType.DMA((depths,)), pltpu.SemaphoreType.DMA((4, depths))
    return [row] * 10 + [square] * 2 + [pltpu.SemaphoreType.DMA]


class Gather:
    def __init__(self, source, result, sems, depths, cut):
        self.source, self.result, self.sems = source, result, sems
        self.depths, self.cut = depths, cut
        self.width = source.shape[-1]

    def along(self, s):
        head, depth, x, core = spot()
        device = at_spot(head, lax.rem(depth + s, self.depths), x, core)
        target = self.result.at[head, depth, x, core]
        return push(self.source, target, self.sems[0].at[s], self.sems[1].at[s], device)

    def block(self, s, far_head, far_x):
        head, depth, x, core = spot()
        return self.result.at[
            1 - head if far_head else head,
            lax.rem(depth - s + self.depths, self.depths),
            1 - x if far_x else x,
            core,
        ]

    def hop(self, kind, s):
        head, depth, x, core = spot()
        if kind in (0, 3):
            device = at_spot(head, depth, 1 - x, core)
        else:
            device = at_spot(1 - head, depth, x, core)
        view = self.block(s, kind == 3, kind == 2)
        if kind == 2:
            view = view.at[:, pl.ds(0, self.cut)]
        if kind == 3:
            view = view.at[:, pl.ds(self.cut, self.width - self.cut)]
        sems = self.sems
        return push(view, view, sems[2 + 2 * kind].at[s], sems[3 + 2 * kind].at[s], device)

    def kinds(self):
        return (2, 3) if self.cut < self.width else (2,)

    def share(self, part, s):
        head, depth, x, core = spot()
        view = self.block(s, part // 2 == 1, part % 2 == 1)
        device = at_spot(head, depth, x, 1 - core)
        return push(view, view, self.sems[10].at[part, s], self.sems[11].at[part, s], device)

    def own(self):
        return pltpu.make_async_copy(self.source, self.result.at[spot()], self.sems[12])

    def start(self):
        self.own().start()
        loop(1, self.depths, lambda s: self.along(s).start())

    def begin_near(self, s):
        self.hop(0, s).start()
        self.hop(1, s).start()
        self.share(0, s).start()

    def start_own(self):
        self.own().wait()
        self.begin_near(0)

    def spread_near(self):
        def step(s):
            self.along(s).wait_recv()
            self.begin_near(s)

        loop(1, self.depths, step)

    def spread_far(self):
        def step(s):
            self.hop(0, s).wait_recv()
            self.hop(2, s).start()
            self.share(1, s).start()
            self.hop(1, s).wait_recv()
            if self.cut < self.width:
                self.hop(3, s).start()
            self.share(2, s).start()

        loop(0, self.depths, step)

    def settle(self):
        def step(s):
            for kind in self.kinds():
                self.hop(kind, s).wait_recv()
            self.share(3, s).start()

        loop(0, self.depths, step)

    def finish(self):
        loop(1, self.depths, lambda s: self.along(s).wait_send())

        def step(s):
            for kind in (0, 1) + self.kinds():
                self.hop(kind, s).wait_send()
            for part in range(4):
                self.share(part, s).wait()

        loop(0, self.depths, step)


def cut_of(width):
    return width // 256 * 128 if width >= 256 else width


def gathered_shape(shard, depths):
    return jax.ShapeDtypeStruct((2, depths, 2, 2) + shard.shape, shard.dtype)


def gather_kernel(depths, count, *refs):
    gathers = gathers_of(refs[:count], refs[count : 2 * count], refs[2 * count :], depths)
    greet_mesh(depths)
    for step in ("start", "start_own", "spread_near", "spread_far", "settle", "finish"):
        for gather in gathers:
            getattr(gather, step)()


def gather_all(arrays, cols, collective_id):
    depths, count = cols // 4, len(arrays)
    return pl.pallas_call(
        functools.partial(gather_kernel, depths, count),
        out_shape=[gathered_shape(array, depths) for array in arrays],
        in_specs=[pl.BlockSpec(memory_space=pl.ANY)] * count,
        out_specs=[pl.BlockSpec(memory_space=pl.ANY)] * count,
        scratch_shapes=gather_sems(depths) * count,
        compiler_params=pltpu.CompilerParams(collective_id=collective_id, has_side_effects=True),
    )(*arrays)


REDUCE_SCRATCH = 20


class Reduce:
    def __init__(self, parts, total, scratch, depths, cut):
        self.parts, self.total = parts, total
        self.sums, self.core_in, self.a1, self.b1, self.a2, self.b2, self.z_in = scratch[:7]
        self.sems = scratch[7:]
        self.depths, self.cut = depths, cut
        self.width = parts.shape[-1]
        self.two = cut < self.width
        self.first = pl.ds(0, cut)
        self.rest = pl.ds(cut, self.width - cut)

    def goal(self, s):
        return lax.rem(spot()[1] + s, self.depths)

    def to_core(self, s):
        head, depth, x, core = spot()
        goal = self.goal(s)
        return push(
            self.parts.at[:, goal, :, 1 - core],
            self.core_in.at[:, goal],
            self.sems[0].at[s],
            self.sems[1].at[s],
            at_spot(head, depth, x, 1 - core),
        )

    def hop(self, kind, s):
        head, depth, x, core = spot()
        goal = self.goal(s)
        over_x = at_spot(head, depth, 1 - x, core)
        over_head = at_spot(1 - head, depth, x, core)
        if kind == 0:
            view = self.sums.at[1 - head, goal, :, :, self.first]
            target, device = self.a1.at[goal], over_head
        elif kind == 1:
            view = self.sums.at[:, goal, 1 - x, :, self.rest]
            target, device = self.b1.at[goal], over_x
        elif kind == 2:
            view = self.sums.at[head, goal, 1 - x, :, self.first]
            target, device = self.a2.at[goal], over_x
        else:
            view = self.sums.at[1 - head, goal, x, :, self.rest]
            target, device = self.b2.at[goal], over_head
        send, recv = self.sems[2 + 2 * kind], self.sems[3 + 2 * kind]
        return push(view, target, send.at[s], recv.at[s], device)

    def along(self, s):
        head, depth, x, core = spot()
        goal = self.goal(s)
        return push(
            self.sums.at[head, goal, x],
            self.z_in.at[s],
            self.sems[10].at[s],
            self.sems[11].at[s],
            at_spot(head, goal, x, core),
        )

    def own(self, s):
        goal = self.goal(s)
        return pltpu.make_async_copy(
            self.parts.at[:, goal, :, spot()[3]], self.sums.at[:, goal], self.sems[12].at[s]
        )

    def start(self):
        def step(s):
            self.to_core(s).start()
            self.own(s).start()

        self.each(step, 0, self.depths)

    def each(self, step, first, last):
        loop(first, last, lambda i: step(lax.rem(i + 1, self.depths)))

    def add(self, where, columns, arrived):
        place = where + (slice(None), columns)
        self.sums[place] = self.sums[place] + arrived

    def near(self, first, last):
        def step(s):
            goal = self.goal(s)
            self.own(s).wait()
            self.to_core(s).wait_recv()
            whole = pl.ds(0, self.width)
            for k in range(4):
                self.add((k // 2, goal, k % 2), whole, self.core_in[k // 2, goal, k % 2])
            self.hop(0, s).start()
            if self.two:
                self.hop(1, s).start()

        self.each(step, first, last)

    def middle(self, first, last):
        head, _, x, _ = spot()

        def step(s):
            goal = self.goal(s)
            self.hop(0, s).wait_recv()
            for k in range(2):
                self.add((head, goal, k), self.first, self.a1[goal, k])
            self.hop(2, s).start()
            if self.two:
                self.hop(1, s).wait_recv()
                for k in range(2):
                    self.add((k, goal, x), self.rest, self.b1[goal, k])
                self.hop(3, s).start()

        self.each(step, first, last)

    def far(self, first, last):
        head, _, x, _ = spot()

        def step(s):
            goal = self.goal(s)
            self.hop(2, s).wait_recv()
            self.add((head, goal, x), self.first, self.a2[goal])
            if self.two:
                self.hop(3, s).wait_recv()
                self.add((head, goal, x), self.rest, self.b2[goal])
            pl.when(s > 0)(lambda: self.along(s).start())

        self.each(step, first, last)

    def finish(self):
        head, depth, x, _ = spot()
        self.total[...] = self.sums[head, depth, x].astype(jnp.float32)

        def step(s):
            self.along(s).wait_recv()
            self.total[...] += self.z_in[s].astype(jnp.float32)

        loop(1, self.depths, step)

        def sent(s):
            self.to_core(s).wait_send()
            for kind in (0, 1, 2, 3) if self.two else (0, 2):
                self.hop(kind, s).wait_send()

        loop(0, self.depths, sent)
        loop(1, self.depths, lambda s: self.along(s).wait_send())


def reduce_scratch(shape, dtype, depths, cut):
    rows, width = shape[-2:]
    rest = max(width - cut, 128)
    row = pltpu.SemaphoreType.DMA((depths,))
    return [
        pltpu.VMEM((2, depths, 2, rows, width), dtype),
        pltpu.VMEM((2, depths, 2, rows, width), dtype),
        pltpu.VMEM((depths, 2, rows, cut), dtype),
        pltpu.VMEM((depths, 2, rows, rest), dtype),
        pltpu.VMEM((depths, rows, cut), dtype),
        pltpu.VMEM((depths, rows, rest), dtype),
        pltpu.VMEM((depths, rows, width), dtype),
    ] + [row] * 13


def reduces_of(parts, totals, scratch, depths):
    return [
        Reduce(
            part,
            totals[i],
            scratch[REDUCE_SCRATCH * i : REDUCE_SCRATCH * (i + 1)],
            depths,
            cut_of(part.shape[-1]),
        )
        for i, part in enumerate(parts)
    ]


def reduce_kernel(depths, count, *refs):
    reduces = reduces_of(refs[:count], refs[count : 2 * count], refs[2 * count :], depths)
    greet_mesh(depths)
    for reduce in reduces:
        reduce.start()
    for step in ("near", "middle", "far"):
        for reduce in reduces:
            getattr(reduce, step)(0, depths)
    for reduce in reduces:
        reduce.finish()


def all_reduce_scratch(arrays, depths):
    scratch = []
    for array in arrays:
        scratch += reduce_scratch(array.shape, array.dtype, depths, cut_of(array.shape[-1]))
    return scratch


def reduce_all(arrays, cols, collective_id):
    depths, count = cols // 4, len(arrays)
    return pl.pallas_call(
        functools.partial(reduce_kernel, depths, count),
        out_shape=[jax.ShapeDtypeStruct(array.shape[-2:], jnp.float32) for array in arrays],
        in_specs=[pl.BlockSpec(memory_space=pl.ANY)] * count,
        out_specs=[pl.BlockSpec(memory_space=pltpu.VMEM)] * count,
        scratch_shapes=all_reduce_scratch(arrays, depths),
        compiler_params=pltpu.CompilerParams(
            collective_id=collective_id, has_side_effects=True, vmem_limit_bytes=52 * 2**20
        ),
    )(*arrays)


def unit_place(pair):
    return lax.rem(pair, 4) != 3, lax.div(pair, 4) * 3 + lax.rem(pair, 4)


def greet_units(cols, pairs, sibling, to_units):
    me = flat_index(cols)
    core, pair = lax.rem(me, 2), lax.div(me, 2)
    holds, unit = unit_place(pair)
    barrier = pltpu.get_barrier_semaphore()
    units = pairs // 4 * 3
    extra = 1 if sibling else 0
    if sibling:
        pl.when(holds)(lambda: greet(me + 1 - 2 * core, cols))
    if to_units:

        @pl.when(holds)
        def _():
            loop(1, pairs, lambda s: greet(lax.rem(pair + s, pairs) * 2 + core, cols))
            pl.semaphore_wait(barrier, units - 1 + extra)

        pl.when(jnp.logical_not(holds))(lambda: pl.semaphore_wait(barrier, units))
    else:

        def to_unit(s):
            other = lax.rem(pair + s, pairs)
            pl.when(unit_place(other)[0])(lambda: greet(other * 2 + core, cols))

        loop(1, pairs, to_unit)
        pl.when(holds)(lambda: pl.semaphore_wait(barrier, pairs - 1 + extra))
    return me, core, pair, holds, unit


def to_units_kernel(cols, pairs, with_kv, *refs):
    if with_kv:
        source, q_out, kv_out, send, recv, own_sem, kv_send, kv_recv, fwd_send, fwd_recv = refs
    else:
        source, q_out, send, recv, own_sem = refs
    me, core, pair, holds, _ = greet_units(cols, pairs, with_kv, True)
    q_rows = pl.ds(0, HEAD_DIM)
    kv_rows = pl.ds(HEAD_DIM, 2 * HEAD_DIM)

    def far(s):
        other = lax.rem(pair + s, pairs)
        unit = unit_place(other)[1]
        target = other * 2 + core
        copies = [
            remote(
                source.at[unit, q_rows] if with_kv else source.at[unit],
                q_out.at[pair],
                send.at[s],
                recv.at[s],
                target,
                cols,
            )
        ]
        if with_kv:
            copies.append(
                remote(
                    source.at[unit, kv_rows],
                    kv_out.at[me],
                    kv_send.at[s],
                    kv_recv.at[s],
                    target,
                    cols,
                )
            )
        return copies

    def own():
        unit = unit_place(pair)[1]
        copies = [
            pltpu.make_async_copy(
                source.at[unit, q_rows] if with_kv else source.at[unit],
                q_out.at[pair],
                own_sem.at[0],
            )
        ]
        if with_kv:
            copies.append(
                pltpu.make_async_copy(source.at[unit, kv_rows], kv_out.at[me], own_sem.at[1])
            )
        return copies

    def forward(s):
        block = kv_out.at[lax.rem(pair - s + pairs, pairs) * 2 + core]
        return remote(block, block, fwd_send.at[s], fwd_recv.at[s], me + 1 - 2 * core, cols)

    def sends(s, action):
        def run():
            for copy in far(s):
                action(copy)

        pl.when(unit_place(lax.rem(pair + s, pairs))[0])(run)

    loop(1, pairs, lambda s: sends(s, lambda copy: copy.start()))

    @pl.when(holds)
    def _():
        for copy in own():
            copy.start()
        for copy in own():
            copy.wait()
        if with_kv:
            forward(0).start()

        def take(s):
            for copy in far(s):
                copy.wait_recv()
            if with_kv:
                forward(s).start()

        loop(1, pairs, take)
        if with_kv:
            loop(0, pairs, lambda s: forward(s).wait())

    loop(1, pairs, lambda s: sends(s, lambda copy: copy.wait_send()))


def to_units(blocks, cols, with_kv, collective_id):
    units, rows, width = blocks.shape
    pairs = units // 3 * 4
    out_shape = [jax.ShapeDtypeStruct((pairs, HEAD_DIM, width), blocks.dtype)]
    scratch = [
        pltpu.SemaphoreType.DMA((pairs,)),
        pltpu.SemaphoreType.DMA((pairs,)),
        pltpu.SemaphoreType.DMA((2,)),
    ]
    if with_kv:
        out_shape.append(jax.ShapeDtypeStruct((2 * pairs, 2 * HEAD_DIM, width), blocks.dtype))
        scratch += [pltpu.SemaphoreType.DMA((pairs,))] * 4
    return pl.pallas_call(
        functools.partial(to_units_kernel, cols, pairs, with_kv),
        out_shape=out_shape,
        in_specs=[pl.BlockSpec(memory_space=pl.ANY)],
        out_specs=[pl.BlockSpec(memory_space=pl.ANY)] * len(out_shape),
        scratch_shapes=scratch,
        compiler_params=pltpu.CompilerParams(collective_id=collective_id, has_side_effects=True),
    )(blocks)


def project_kernel(
    cols, x_ref, gain_ref, w_ref, cos_ref, sin_ref, normed_ref, scale_ref, q_out, kv_out,
    stage, q_send, q_recv, kv_send, kv_recv, fwd_send, fwd_recv, own_sem,
):
    me = flat_index(cols)
    core, pair = lax.rem(me, 2), lax.div(me, 2)
    holds, unit = unit_place(pair)
    sibling = me + 1 - 2 * core
    pairs, heads = q_out.shape[0], stage.shape[0]
    barrier = pltpu.get_barrier_semaphore()
    width = heads * HEAD_DIM

    @pl.when(holds)
    def _():
        loop(1, pairs, lambda s: greet(lax.rem(pair + s, pairs) * 2 + core, cols))
        greet(sibling, cols)

    rows = x_ref[...]
    scale = lax.rsqrt(jnp.mean(rows * rows, axis=-1, keepdims=True) + EPSILON)
    normed = (rows * scale * gain_ref[...]).astype(jnp.bfloat16)
    scale_ref[...] = scale
    normed_ref[...] = normed
    cosine, sine = cos_ref[...], sin_ref[...]
    half = HEAD_DIM // 2
    q_rows, kv_rows = pl.ds(0, HEAD_DIM), pl.ds(HEAD_DIM, 2 * HEAD_DIM)

    def q_far(u, holder):
        return remote(
            stage.at[u, q_rows], q_out.at[pair], q_send.at[u], q_recv.at[pair], holder * 2 + core,
            cols,
        )

    def kv_far(u, holder):
        return remote(
            stage.at[u, kv_rows], kv_out.at[me], kv_send.at[u], kv_recv.at[pair],
            holder * 2 + core, cols,
        )

    q_own = pltpu.make_async_copy(stage.at[unit, q_rows], q_out.at[pair], own_sem.at[0])
    kv_own = pltpu.make_async_copy(stage.at[unit, kv_rows], kv_out.at[me], own_sem.at[1])

    def forward(source):
        block = kv_out.at[source * 2 + core]
        return remote(block, block, fwd_send.at[source], fwd_recv.at[source], sibling, cols)

    per = TILE // HEAD_DIM
    for group in range(heads // per):
        for part in range(3):
            at = pl.ds(part * width + group * TILE, TILE)
            turned = dot(normed, w_ref[:, at], (1, 0)).T
            for k in range(per):
                head = group * per + k
                low = part * HEAD_DIM
                block = turned[k * HEAD_DIM : (k + 1) * HEAD_DIM]
                if part < 2:
                    first, second = block[:half], block[half:]
                    block = jnp.concatenate(
                        [first * cosine - second * sine, second * cosine + first * sine], axis=0
                    )
                stage[head, low : low + HEAD_DIM, :] = block.astype(jnp.bfloat16)
        if group == 0:
            pl.when(holds)(lambda: pl.semaphore_wait(barrier, heads))
            pl.when(jnp.logical_not(holds))(lambda: pl.semaphore_wait(barrier, heads))
        for k in range(per):
            u = group * per + k
            holder = u // 3 * 4 + u % 3

            @pl.when(pair != holder)
            def _(u=u, holder=holder):
                kv_far(u, holder).start()
                q_far(u, holder).start()

            @pl.when(pair == holder)
            def _():
                kv_own.start()
                q_own.start()

    @pl.when(holds)
    def _():
        kv_own.wait()
        forward(pair).start()

        def take(s):
            source = lax.rem(pair - s + pairs, pairs)
            arrival = remote(
                stage.at[unit, kv_rows], kv_out.at[source * 2 + core], kv_send.at[unit],
                kv_recv.at[source], source * 2 + core, cols,
            )
            arrival.wait_recv()
            forward(source).start()

        loop(1, pairs, take)

        def take_q(s):
            source = lax.rem(pair - s + pairs, pairs)
            remote(
                stage.at[unit, q_rows], q_out.at[source], q_send.at[unit], q_recv.at[source],
                source * 2 + core, cols,
            ).wait_recv()

        loop(1, pairs, take_q)
        loop(0, pairs, lambda source: forward(source).wait())
        q_own.wait()

    def sent(u, holder):
        kv_far(u, holder).wait_send()
        q_far(u, holder).wait_send()

    other_units(pairs, pair, sent)


def project(rows, gain, weights, cosine, sine, cols, collective_id):
    tokens, width = rows.shape
    heads = width // HEAD_DIM
    pairs = heads // 3 * 4
    by_pair, by_unit = pltpu.SemaphoreType.DMA((pairs,)), pltpu.SemaphoreType.DMA((heads,))
    vmem = pl.BlockSpec(memory_space=pltpu.VMEM)
    everywhere = pl.BlockSpec(memory_space=pl.ANY)
    return pl.pallas_call(
        functools.partial(project_kernel, cols),
        out_shape=[
            jax.ShapeDtypeStruct((tokens, width), jnp.bfloat16),
            jax.ShapeDtypeStruct((tokens, 1), jnp.float32),
            jax.ShapeDtypeStruct((pairs, HEAD_DIM, tokens), jnp.bfloat16),
            jax.ShapeDtypeStruct((2 * pairs, 2 * HEAD_DIM, tokens), jnp.bfloat16),
        ],
        in_specs=[vmem] * 5,
        out_specs=[vmem, vmem, everywhere, everywhere],
        scratch_shapes=[
            pltpu.VMEM((heads, 3 * HEAD_DIM, tokens), jnp.bfloat16),
            by_unit,
            by_pair,
            by_unit,
            by_pair,
            by_pair,
            by_pair,
            pltpu.SemaphoreType.DMA((2,)),
        ],
        compiler_params=pltpu.CompilerParams(
            collective_id=collective_id, has_side_effects=True, vmem_limit_bytes=40 * 2**20
        ),
    )(rows, gain.reshape(1, width), weights, cosine, sine)


def to_tokens_kernel(cols, pairs, with_kv, *refs):
    if with_kv:
        q_in, kv_in, q_out, kv_out, send, recv, own_sem = refs[:7]
        stage, inbox, kv_send, kv_recv, near_send, near_recv = refs[7:]
    else:
        q_in, q_out, send, recv, own_sem = refs
    me, core, pair, holds, unit = greet_units(cols, pairs, with_kv, False)

    def far(s):
        other = lax.rem(pair + s, pairs)
        target = other * 2 + core
        copies = [remote(q_in.at[other], q_out.at[unit], send.at[s], recv.at[s], target, cols)]
        if with_kv:
            copies.append(
                remote(
                    stage.at[other], kv_out.at[unit], kv_send.at[s], kv_recv.at[s], target, cols
                )
            )
        return copies

    def own():
        copies = [pltpu.make_async_copy(q_in.at[pair], q_out.at[unit], own_sem.at[0])]
        if with_kv:
            copies.append(pltpu.make_async_copy(stage.at[pair], kv_out.at[unit], own_sem.at[1]))
        return copies

    def near(s):
        other = lax.rem(pair + s, pairs)
        return remote(
            kv_in.at[other * 2 + 1 - core],
            inbox.at[other],
            near_send.at[s],
            near_recv.at[s],
            me + 1 - 2 * core,
            cols,
        )

    def add(s):
        other = lax.rem(pair + s, pairs)
        total = kv_in[other * 2 + core].astype(jnp.float32) + inbox[other].astype(jnp.float32)
        stage[other] = total.astype(stage.dtype)

    @pl.when(holds)
    def _():
        if with_kv:
            loop(1, pairs, lambda s: near(s).start())
            near(0).start()

        def give(s):
            if with_kv:
                near(s).wait_recv()
                add(s)
            for copy in far(s):
                copy.start()

        loop(1, pairs, give)
        if with_kv:
            near(0).wait_recv()
            add(0)
        for copy in own():
            copy.start()
        for copy in own():
            copy.wait()

    def take(s):
        def run():
            for copy in far(s):
                copy.wait_recv()

        pl.when(unit_place(lax.rem(pair - s + pairs, pairs))[0])(run)

    loop(1, pairs, take)

    @pl.when(holds)
    def _():
        def sent(s):
            for copy in far(s):
                copy.wait_send()

        loop(1, pairs, sent)
        if with_kv:
            loop(0, pairs, lambda s: near(s).wait_send())


def to_tokens(arrays, cols, collective_id):
    with_kv = len(arrays) == 2
    pairs, _, width = arrays[0].shape
    units = pairs // 4 * 3
    out_shape = [jax.ShapeDtypeStruct((units, HEAD_DIM, width), arrays[0].dtype)]
    in_specs = [pl.BlockSpec(memory_space=pl.ANY)]
    scratch = [
        pltpu.SemaphoreType.DMA((pairs,)),
        pltpu.SemaphoreType.DMA((pairs,)),
        pltpu.SemaphoreType.DMA((2,)),
    ]
    if with_kv:
        out_shape.append(jax.ShapeDtypeStruct((units, 2 * HEAD_DIM, width), arrays[1].dtype))
        in_specs.append(pl.BlockSpec(memory_space=pltpu.VMEM))
        scratch += [pltpu.VMEM((pairs, 2 * HEAD_DIM, width), arrays[1].dtype)] * 2
        scratch += [pltpu.SemaphoreType.DMA((pairs,))] * 4
    return pl.pallas_call(
        functools.partial(to_tokens_kernel, cols, pairs, with_kv),
        out_shape=out_shape,
        in_specs=in_specs,
        out_specs=[pl.BlockSpec(memory_space=pl.ANY)] * len(out_shape),
        scratch_shapes=scratch,
        compiler_params=pltpu.CompilerParams(
            collective_id=collective_id, has_side_effects=True, vmem_limit_bytes=48 * 2**20
        ),
    )(*arrays)


def wide_of(first, blocks):
    return pl.ds(pl.multiple_of(first * TILE, TILE), blocks * TILE)


def in_reach(first, shape, place, run):
    key_pos = first * TILE + lax.broadcasted_iota(jnp.int32, shape, 0)
    return (key_pos <= place) & (key_pos >= run)


def tile_reach(tile, core, width, wide, masked, blocks):
    joined = TILE // width
    low = (2 * tile * joined + core) * width
    high = low + (2 * joined - 1) * width - 1
    prompt = low < PROMPT
    full = jnp.where(prompt, low // (TILE * wide), PROMPT // (TILE * wide))
    back = jnp.maximum((low - LONGEST + 1) // TILE, PROMPT // TILE)
    first = jnp.where(prompt, full * wide, back)
    steps = (high // TILE + masked - first) // masked
    first = jnp.minimum(first, blocks - steps * masked)
    lane = lax.broadcasted_iota(jnp.int32, (1, TILE), 1)
    place = low + lane + lane // width * width
    return full, first, steps, place


CHUNK = 64


def fill_rows(kv_ref, first_row, rows):
    def fill(b):
        rows[wide_of(b, 1), :] = kv_ref[b, first_row : first_row + HEAD_DIM, :].T

    loop(0, kv_ref.shape[0], fill)


def forward_tile(tile, core, width, queries, run, kv_ref, key_rows, kept):
    full, start, steps, place = tile_reach(
        tile, core, width, FWD_WIDE, FWD_MASK, kv_ref.shape[0]
    )

    def by_eight(value):
        return value.reshape(-1, 8, TILE)

    def fold(blocks, first, state, masked):
        top, total, gathered = state
        base = pl.multiple_of(first * TILE, TILE)
        highest = top
        for c in range(blocks * TILE // CHUNK):
            scores = jnp.dot(
                key_rows[pl.ds(base + c * CHUNK, CHUNK), :],
                queries,
                preferred_element_type=jnp.float32,
            )
            if masked:
                key_pos = base + c * CHUNK + lax.broadcasted_iota(jnp.int32, scores.shape, 0)
                scores = jnp.where((key_pos <= place) & (key_pos >= run), scores, NEGATIVE)
            kept[c * CHUNK : (c + 1) * CHUNK, :] = scores
            highest = jnp.maximum(highest, jnp.max(by_eight(scores), axis=0))
        new_top = jnp.broadcast_to(jnp.max(highest, axis=0, keepdims=True), (8, TILE))
        shrink = jnp.exp2((top - new_top) * EXP_SCALE)
        total = total * shrink
        gathered = (by_eight(gathered) * shrink[None]).reshape(HEAD_DIM, TILE)
        for j in range(blocks):
            low = []
            for c in range(j * TILE // CHUNK, (j + 1) * TILE // CHUNK):
                scores = by_eight(kept[c * CHUNK : (c + 1) * CHUNK, :])
                weights = jnp.exp2((scores - new_top[None]) * EXP_SCALE)
                total = total + jnp.sum(weights, axis=0)
                low.append(weights.reshape(CHUNK, TILE).astype(jnp.bfloat16))
            gathered = gathered + jnp.dot(
                kv_ref[first + j, HEAD_DIM : 2 * HEAD_DIM, :],
                jnp.concatenate(low, axis=0),
                preferred_element_type=jnp.float32,
            )
        return (new_top, total, gathered)

    state = (
        jnp.full((8, TILE), NEGATIVE, jnp.float32),
        jnp.zeros((8, TILE), jnp.float32),
        jnp.zeros((HEAD_DIM, TILE), jnp.float32),
    )
    state = lax.fori_loop(0, full, lambda b, s: fold(FWD_WIDE, b * FWD_WIDE, s, False), state)
    top, total, gathered = lax.fori_loop(
        0, steps, lambda b, s: fold(FWD_MASK, start + b * FWD_MASK, s, True), state
    )
    total = jnp.sum(total, axis=0, keepdims=True)
    exact = gathered / total
    return exact, exact.astype(jnp.bfloat16), top[0:1] * EXP_SCALE + jnp.log2(total)


def forward_scratch(blocks):
    return [
        pltpu.VMEM((blocks * TILE, HEAD_DIM), jnp.bfloat16),
        pltpu.VMEM((max(FWD_WIDE, FWD_MASK) * TILE, TILE), jnp.float32),
    ]


def my_unit():
    me = flat_index(lax.axis_size("blk"))
    pair = lax.div(me, 2)
    holds, unit = unit_place(pair)
    return me, lax.rem(me, 2), pair, holds, unit


def forward_kernel(width, q_ref, kv_ref, run_ref, o_ref, ob_ref, lse_ref, key_rows, kept):
    tile = pl.program_id(0)
    _, core, _, holds, _ = my_unit()

    @pl.when(holds & (tile == 0))
    def _():
        fill_rows(kv_ref, 0, key_rows)

    @pl.when(holds)
    def _():
        o_ref[0], ob_ref[0], lse_ref[0] = forward_tile(
            tile, core, width, q_ref[0], run_ref[0], kv_ref, key_rows, kept
        )


def tile_spec(rows):
    return pl.BlockSpec((1, rows, TILE), lambda i: (i, 0, 0))


def attend(queries, keys_values, run, width):
    tiles = queries.shape[0]
    held = pl.BlockSpec(keys_values.shape, lambda i: (0, 0, 0))
    return pl.pallas_call(
        functools.partial(forward_kernel, width),
        grid=(tiles,),
        in_specs=[tile_spec(HEAD_DIM), held, tile_spec(1)],
        out_specs=[tile_spec(HEAD_DIM), tile_spec(HEAD_DIM), tile_spec(1)],
        scratch_shapes=forward_scratch(keys_values.shape[0]),
        out_shape=[
            jax.ShapeDtypeStruct((tiles, HEAD_DIM, TILE), jnp.float32),
            jax.ShapeDtypeStruct((tiles, HEAD_DIM, TILE), jnp.bfloat16),
            jax.ShapeDtypeStruct((tiles, 1, TILE), jnp.float32),
        ],
        compiler_params=pltpu.CompilerParams(vmem_limit_bytes=48 * 2**20),
    )(queries, keys_values, run)


def other_units(pairs, pair, action):
    def one(u):
        holder = lax.div(u, 3) * 4 + lax.rem(u, 3)
        pl.when(holder != pair)(lambda: action(u, holder))

    loop(0, pairs // 4 * 3, one)


def gathers_of(sources, results, sems, depths):
    return [
        Gather(
            source,
            results[i],
            sems[GATHER_SEMS * i : GATHER_SEMS * (i + 1)],
            depths,
            cut_of(source.shape[-1]),
        )
        for i, source in enumerate(sources)
    ]


GATHER_AT = {"start": 0, "start_own": 0, "spread_near": 7, "spread_far": 10, "settle": 13}


def forward_home_kernel(cols, count, *refs):
    q_ref, kv_ref, run_ref = refs[:3]
    sources, refs = refs[3 : 3 + count], refs[3 + count :]
    o_ref, lse_ref, home = refs[:3]
    results, refs = refs[3 : 3 + count], refs[3 + count :]
    key_rows, kept, low, send, recv, own_sem = refs[:6]
    gathers = gathers_of(sources, results, refs[6:], cols // 4)
    tile, tiles = pl.program_id(0), tiles_of(kv_ref)
    me, core, pair, holds, unit = my_unit()

    @pl.when(tile == 0)
    def _():
        loop(1, tiles, lambda s: greet(lax.rem(pair + s, tiles) * 2 + core, cols))
        greet(me + 1 - 2 * core, cols)

    @pl.when(holds & (tile == 0))
    def _():
        fill_rows(kv_ref, 0, key_rows)

    @pl.when(tile == 0)
    def _():
        pl.semaphore_wait(pltpu.get_barrier_semaphore(), tiles)

    for name, place_at in GATHER_AT.items():

        @pl.when(tile == place_at)
        def _(name=name):
            for gather in gathers:
                getattr(gather, name)()

    def away(t):
        return remote(
            low.at[t], home.at[unit], send.at[t], recv.at[unit], t * 2 + core, cols
        )

    stays = pltpu.make_async_copy(low.at[pair], home.at[unit], own_sem)

    @pl.when(holds)
    def _():
        o_ref[0], low[tile], lse_ref[0] = forward_tile(
            tile, core, TILE, q_ref[0], run_ref[0], kv_ref, key_rows, kept
        )
        pl.when(tile != pair)(lambda: away(tile).start())
        pl.when(tile == pair)(lambda: stays.start())

    @pl.when(tile == tiles - 1)
    def _():
        for gather in gathers:
            gather.finish()

        def arrived(u, holder):
            remote(
                low.at[pair], home.at[u], send.at[pair], recv.at[u], holder * 2 + core, cols
            ).wait_recv()

        other_units(tiles, pair, arrived)

        @pl.when(holds)
        def _():
            def sent(t):
                pl.when(t != pair)(lambda: away(t).wait_send())

            loop(0, tiles, sent)
            stays.wait()


def tiles_of(kv_ref):
    return kv_ref.shape[0] // 2


def attend_home(queries, keys_values, run, shards, cols, collective_id):
    tiles, units, depths = queries.shape[0], queries.shape[0] // 4 * 3, cols // 4
    held = pl.BlockSpec(keys_values.shape, lambda i: (0, 0, 0))
    everywhere = pl.BlockSpec(memory_space=pl.ANY)
    return pl.pallas_call(
        functools.partial(forward_home_kernel, cols, len(shards)),
        grid=(tiles,),
        in_specs=[tile_spec(HEAD_DIM), held, tile_spec(1)] + [everywhere] * len(shards),
        out_specs=[tile_spec(HEAD_DIM), tile_spec(1), everywhere] + [everywhere] * len(shards),
        scratch_shapes=forward_scratch(keys_values.shape[0])
        + [
            pltpu.VMEM((tiles, HEAD_DIM, TILE), jnp.bfloat16),
            pltpu.SemaphoreType.DMA((tiles,)),
            pltpu.SemaphoreType.DMA((units,)),
            pltpu.SemaphoreType.DMA,
        ]
        + gather_sems(depths) * len(shards),
        out_shape=[
            jax.ShapeDtypeStruct((tiles, HEAD_DIM, TILE), jnp.float32),
            jax.ShapeDtypeStruct((tiles, 1, TILE), jnp.float32),
            jax.ShapeDtypeStruct((units, HEAD_DIM, TILE), jnp.bfloat16),
        ]
        + [gathered_shape(shard, depths) for shard in shards],
        compiler_params=pltpu.CompilerParams(
            collective_id=collective_id, has_side_effects=True, vmem_limit_bytes=48 * 2**20
        ),
    )(queries, keys_values, run, *shards)


def backward_tile(
    tile, core, width, queries, grads, exact, lse, run,
    kv_ref, key_rows, value_rows, dk_sum, dv_sum,
):
    full, start, steps, place = tile_reach(
        tile, core, width, BWD_WIDE, BWD_MASK, kv_ref.shape[0]
    )
    delta = jnp.sum(grads.astype(jnp.float32) * exact, axis=0, keepdims=True)
    over_queries = (((1,), (1,)), ((), ()))

    def fold(blocks, first, dq, masked):
        rows = wide_of(first, blocks)
        scores = jnp.dot(key_rows[rows, :], queries, preferred_element_type=jnp.float32)
        probs = jnp.exp2(scores * EXP_SCALE - lse)
        if masked:
            probs = jnp.where(in_reach(first, scores.shape, place, run), probs, 0.0)
        dp = jnp.dot(value_rows[rows, :], grads, preferred_element_type=jnp.float32)
        ds = (probs * (dp - delta)).astype(jnp.bfloat16)
        low = probs.astype(jnp.bfloat16)
        for j in range(blocks):
            part = slice(j * TILE, (j + 1) * TILE)
            dv_sum[first + j] += lax.dot_general(
                grads, low[part], over_queries, preferred_element_type=jnp.float32
            )
            dk_sum[first + j] += lax.dot_general(
                queries, ds[part], over_queries, preferred_element_type=jnp.float32
            )
            dq = dq + jnp.dot(
                kv_ref[first + j, 0:HEAD_DIM, :], ds[part], preferred_element_type=jnp.float32
            )
        return dq

    dq = jnp.zeros((HEAD_DIM, TILE), jnp.float32)
    dq = lax.fori_loop(0, full, lambda b, s: fold(BWD_WIDE, b * BWD_WIDE, s, False), dq)
    dq = lax.fori_loop(0, steps, lambda b, s: fold(BWD_MASK, start + b * BWD_MASK, s, True), dq)
    return (dq * SCORE_SCALE).astype(jnp.bfloat16)


def backward_begin(kv_ref, key_rows, value_rows, dk_sum, dv_sum):
    fill_rows(kv_ref, 0, key_rows)
    fill_rows(kv_ref, HEAD_DIM, value_rows)

    def clear(b):
        dk_sum[b] = jnp.zeros((HEAD_DIM, TILE), jnp.float32)
        dv_sum[b] = jnp.zeros((HEAD_DIM, TILE), jnp.float32)

    loop(0, kv_ref.shape[0], clear)


def backward_end(dk_sum, dv_sum, dkv, first, last):
    def drain(b):
        dkv[b, 0:HEAD_DIM, :] = (dk_sum[b] * SCORE_SCALE).astype(jnp.bfloat16)
        dkv[b, HEAD_DIM : 2 * HEAD_DIM, :] = dv_sum[b].astype(jnp.bfloat16)

    loop(first, last, drain)


def backward_scratch(blocks):
    return [pltpu.VMEM((blocks * TILE, HEAD_DIM), jnp.bfloat16)] * 2 + [
        pltpu.VMEM((blocks, HEAD_DIM, TILE), jnp.float32)
    ] * 2


NEAR_AT, MIDDLE_AT, FAR_AT = (0, 2, 4, 6), (2, 4, 6, 8), (3, 5, 7, 9)


def reduce_at(step, reduces, depths):
    quarter = depths // 4
    for name, places in (("far", FAR_AT), ("middle", MIDDLE_AT), ("near", NEAR_AT)):
        for part, place_at in enumerate(places):

            @pl.when(step == place_at)
            def _(name=name, part=part):
                for reduce in reduces:
                    getattr(reduce, name)(part * quarter, (part + 1) * quarter)


def backward_kernel(width, depths, count, *refs):
    q_ref, kv_ref, do_ref, o_ref, lse_ref, run_ref = refs[:6]
    parts, refs = refs[6 : 6 + count], refs[6 + count :]
    dq_ref, dkv_ref = refs[:2]
    totals, refs = refs[2 : 2 + count], refs[2 + count :]
    held = refs[:4]
    reduces = reduces_of(parts, totals, refs[4:], depths)
    tile, tiles = pl.program_id(0), pl.num_programs(0)
    _, core, _, holds, _ = my_unit()

    @pl.when(tile == 0)
    def _():
        greet_mesh(depths)
        for reduce in reduces:
            reduce.start()

    reduce_at(tile, reduces, depths)

    @pl.when(holds & (tile == 0))
    def _():
        backward_begin(kv_ref, *held)

    @pl.when(holds)
    def _():
        dq_ref[0] = backward_tile(
            tile, core, width, q_ref[0], do_ref[0], o_ref[0], lse_ref[0], run_ref[0],
            kv_ref, *held,
        )

    @pl.when(holds & (tile == tiles - 1))
    def _():
        backward_end(held[2], held[3], dkv_ref, 0, dkv_ref.shape[0])

    @pl.when(tile == tiles - 1)
    def _():
        for reduce in reduces:
            reduce.finish()


def attend_back(queries, keys_values, grads, exact, lse, run, width, parts, cols, collective_id):
    tiles, blocks = queries.shape[0], keys_values.shape[0]
    held = pl.BlockSpec(keys_values.shape, lambda i: (0, 0, 0))
    wide, flat = tile_spec(HEAD_DIM), tile_spec(1)
    depths = cols // 4
    return pl.pallas_call(
        functools.partial(backward_kernel, width, depths, len(parts)),
        grid=(tiles,),
        in_specs=[wide, held, wide, wide, flat, flat]
        + [pl.BlockSpec(memory_space=pl.ANY)] * len(parts),
        out_specs=[wide, held]
        + [pl.BlockSpec(part.shape[-2:], lambda i: (0, 0)) for part in parts],
        scratch_shapes=backward_scratch(blocks) + all_reduce_scratch(parts, depths),
        out_shape=[
            jax.ShapeDtypeStruct(queries.shape, jnp.bfloat16),
            jax.ShapeDtypeStruct(keys_values.shape, jnp.bfloat16),
        ]
        + [jax.ShapeDtypeStruct(part.shape[-2:], jnp.float32) for part in parts],
        compiler_params=pltpu.CompilerParams(
            collective_id=collective_id, has_side_effects=True, vmem_limit_bytes=52 * 2**20
        ),
    )(queries, keys_values, grads, exact, lse, run, *parts)


def backward_home_kernel(cols, depths, count, *refs):
    q_ref, kv_ref, o_ref, lse_ref, run_ref, do_source = refs[:6]
    parts, refs = refs[6 : 6 + count], refs[6 + count :]
    q_home, kv_home = refs[:2]
    totals, refs = refs[2 : 2 + count], refs[2 + count :]
    held, refs = refs[:4], refs[4:]
    grads, low, dkv, inbox, refs = refs[0], refs[1], refs[2], refs[3], refs[4:]
    in_send, in_recv, q_send, q_recv, kv_send, kv_recv, near_send, near_recv, own_sem = refs[:9]
    reduces = reduces_of(parts, totals, refs[9:], depths)
    step, pairs = pl.program_id(0), tiles_of(kv_ref)
    tile = pairs - 1 - step
    me, core, pair, holds, unit = my_unit()
    sibling = me + 1 - 2 * core
    last = tile == 0

    def do_out(u, holder):
        return remote(
            do_source.at[u], grads.at[pair], in_send.at[u], in_recv.at[pair], holder * 2 + core, cols
        )

    def do_in(t):
        return remote(
            do_source.at[unit], grads.at[t], in_send.at[unit], in_recv.at[t], t * 2 + core, cols
        )

    def q_away(t):
        return remote(low.at[t], q_home.at[unit], q_send.at[t], q_recv.at[unit], t * 2 + core, cols)

    def kv_away(t):
        return remote(
            inbox.at[t], kv_home.at[unit], kv_send.at[t], kv_recv.at[unit], t * 2 + core, cols
        )

    def near(t):
        return remote(
            dkv.at[t * 2 + 1 - core], inbox.at[t], near_send.at[t], near_recv.at[t], sibling, cols
        )

    do_own = pltpu.make_async_copy(do_source.at[unit], grads.at[pair], own_sem.at[0])
    q_stays = pltpu.make_async_copy(low.at[pair], q_home.at[unit], own_sem.at[1])
    kv_stays = pltpu.make_async_copy(inbox.at[pair], kv_home.at[unit], own_sem.at[2])

    def give(t):
        near(t).wait_recv()
        inbox[t] = dkv[t * 2 + core] + inbox[t]
        pl.when(t != pair)(lambda: kv_away(t).start())
        pl.when(t == pair)(lambda: kv_stays.start())

    @pl.when(step == 0)
    def _():
        loop(1, pairs, lambda s: greet(lax.rem(pair + s, pairs) * 2 + core, cols))
        greet(sibling, cols)
        pl.semaphore_wait(pltpu.get_barrier_semaphore(), pairs)
        other_units(pairs, pair, lambda u, holder: do_out(u, holder).start())
        pl.when(holds)(lambda: do_own.start())
        for reduce in reduces:
            reduce.start()

    @pl.when(holds & (step == 0))
    def _():
        backward_begin(kv_ref, *held)

    reduce_at(step, reduces, depths)

    @pl.when(holds)
    def _():
        pl.when(tile != pair)(lambda: do_in(tile).wait_recv())
        pl.when(tile == pair)(lambda: do_own.wait())
        low[tile] = backward_tile(
            tile, core, TILE, q_ref[0], grads[tile], o_ref[0], lse_ref[0], run_ref[0],
            kv_ref, *held,
        )
        pl.when(tile != pair)(lambda: q_away(tile).start())
        pl.when(tile == pair)(lambda: q_stays.start())
        backward_end(held[2], held[3], dkv, 2 * tile, 2 * tile + 2)
        near(tile).start()
        pl.when(step > 0)(lambda: give(tile + 1))
        pl.when(last)(lambda: give(tile))

    @pl.when(last)
    def _():
        for reduce in reduces:
            reduce.finish()

        def arrived(u, holder):
            target = holder * 2 + core
            remote(
                low.at[pair], q_home.at[u], q_send.at[pair], q_recv.at[u], target, cols
            ).wait_recv()
            remote(
                inbox.at[pair], kv_home.at[u], kv_send.at[pair], kv_recv.at[u], target, cols
            ).wait_recv()

        other_units(pairs, pair, arrived)
        other_units(pairs, pair, lambda u, holder: do_out(u, holder).wait_send())

        @pl.when(holds)
        def _():
            def sent(t):
                near(t).wait_send()

                @pl.when(t != pair)
                def _():
                    q_away(t).wait_send()
                    kv_away(t).wait_send()

            loop(0, pairs, sent)
            q_stays.wait()
            kv_stays.wait()


def attend_back_home(queries, keys_values, do_blocks, exact, lse, run, parts, cols, collective_id):
    tiles, blocks = queries.shape[0], keys_values.shape[0]
    units, depths = do_blocks.shape[0], cols // 4
    held = pl.BlockSpec(keys_values.shape, lambda i: (0, 0, 0))
    wide = pl.BlockSpec((1, HEAD_DIM, TILE), lambda i: (tiles - 1 - i, 0, 0))
    flat = pl.BlockSpec((1, 1, TILE), lambda i: (tiles - 1 - i, 0, 0))
    everywhere = pl.BlockSpec(memory_space=pl.ANY)
    by_tile, by_unit = pltpu.SemaphoreType.DMA((tiles,)), pltpu.SemaphoreType.DMA((units,))
    tile_rows = pltpu.VMEM((tiles, HEAD_DIM, TILE), jnp.bfloat16)
    return pl.pallas_call(
        functools.partial(backward_home_kernel, cols, depths, len(parts)),
        grid=(tiles,),
        in_specs=[wide, held, wide, flat, flat, everywhere] + [everywhere] * len(parts),
        out_specs=[everywhere, everywhere]
        + [pl.BlockSpec(part.shape[-2:], lambda i: (0, 0)) for part in parts],
        scratch_shapes=backward_scratch(blocks)
        + [
            tile_rows,
            tile_rows,
            pltpu.VMEM((blocks, 2 * HEAD_DIM, TILE), jnp.bfloat16),
            pltpu.VMEM((tiles, 2 * HEAD_DIM, TILE), jnp.bfloat16),
            by_unit,
            by_tile,
            by_tile,
            by_unit,
            by_tile,
            by_unit,
            by_tile,
            by_tile,
            pltpu.SemaphoreType.DMA((3,)),
        ]
        + all_reduce_scratch(parts, depths),
        out_shape=[
            jax.ShapeDtypeStruct((units, HEAD_DIM, TILE), jnp.bfloat16),
            jax.ShapeDtypeStruct((units, 2 * HEAD_DIM, TILE), jnp.bfloat16),
        ]
        + [jax.ShapeDtypeStruct(part.shape[-2:], jnp.float32) for part in parts],
        compiler_params=pltpu.CompilerParams(
            collective_id=collective_id, has_side_effects=True, vmem_limit_bytes=52 * 2**20
        ),
    )(queries, keys_values, exact, lse, run, do_blocks, *parts)


def to_tiles(blocks):
    count, rows, width = blocks.shape
    if width == TILE:
        return blocks
    joined = TILE // width
    return (
        blocks.reshape(count // joined, joined, rows, width)
        .transpose(0, 2, 1, 3)
        .reshape(count // joined, rows, TILE)
    )


def from_tiles(tiles, width):
    count, rows, _ = tiles.shape
    if width == TILE:
        return tiles
    joined = TILE // width
    return (
        tiles.reshape(count, rows, joined, width)
        .transpose(0, 2, 1, 3)
        .reshape(count * joined, rows, width)
    )


def dot(left, right, over):
    return lax.dot_general(
        left, right, (((over[0],), (over[1],)), ((), ())), preferred_element_type=jnp.float32
    )


STRIP = 512


def strips(total, body):
    width = min(total, STRIP)
    loop(0, total // width, lambda j: body(pl.ds(pl.multiple_of(j * width, width), width)))


def shared_forward(ins, outs, done):
    normed, wide, down = ins
    gate_in, up_in, hidden_low, total = outs
    hidden = down.shape[0]

    def strip(at):
        after = pl.ds(at.start + hidden, at.size)
        gate = dot(normed[...], wide[:, at], (1, 0))
        up = dot(normed[...], wide[:, after], (1, 0))
        gate_in[:, at] = gate.astype(jnp.bfloat16)
        up_in[:, at] = up.astype(jnp.bfloat16)
        hidden_low[:, at] = (apply_silu(gate) * up).astype(jnp.bfloat16)

    strips(hidden, strip)
    for start in done[:3]:
        start()
    total[...] = dot(hidden_low[...], down[...], (1, 0))
    done[3]()


def shared_backward(ins, outs, done):
    grads, normed, gate_in, up_in, hidden_low, wide, down = ins
    grad_wide, grad_down, back = outs
    hidden = down.shape[0]
    normed_t = normed[...].T
    back[...] = jnp.zeros_like(back)

    def strip(at):
        after = pl.ds(at.start + hidden, at.size)
        upstream = dot(grads[...], down[at, :], (1, 1))
        gate, up = gate_in[:, at].astype(jnp.float32), up_in[:, at].astype(jnp.float32)
        low_gate = (upstream * up * silu_slope(gate)).astype(jnp.bfloat16)
        low_up = (upstream * apply_silu(gate)).astype(jnp.bfloat16)
        back[...] += dot(low_gate, wide[:, at], (1, 1)) + dot(low_up, wide[:, after], (1, 1))
        grad_wide[:, at] = dot(normed_t, low_gate, (1, 0)).astype(jnp.bfloat16)
        grad_wide[:, after] = dot(normed_t, low_up, (1, 0)).astype(jnp.bfloat16)
        grad_down[at, :] = dot(hidden_low[:, at].T, grads[...], (1, 0)).astype(jnp.bfloat16)

    strips(hidden, strip)
    for start in done:
        start()


QUARTERS = 4


def quarter_order(pair, per):
    own = lax.div(pair, per)
    outer, inner = lax.div(own, 2), lax.rem(own, 2)
    return [own, (1 - outer) * 2 + inner, outer * 2 + 1 - inner, (1 - outer) * 2 + 1 - inner]


def expert_kernel(cols, step, final, work_first, work, shapes, *refs):
    held_in, held_out, extra = shapes
    sending, refs = refs[0], refs[1:]
    inputs, refs = refs[:held_in], refs[held_in:]
    extra_in = len(work.arrays)
    work_in, refs = refs[:extra_in], refs[extra_in:]
    returned, refs = refs[0], refs[1:]
    outputs, refs = refs[:held_out], refs[held_out:]
    work_out, refs = refs[: len(work.out_shape)], refs[len(work.out_shape) :]
    land, partial, inbox, refs = refs[0], refs[1], refs[2], refs[3:]
    send, recv, share_send, share_recv, near_send, near_recv, refs = refs[:6] + (refs[6:],)
    back_send, back_recv, own_sem, load_sem, refs = refs[:4] + (refs[4:],)
    held, refs = refs[:held_in], refs[held_in:]
    scratch, refs = refs[:extra], refs[extra:]
    begin, run, end = work.bind(work_in + work_out + refs)

    me = flat_index(cols)
    core, pair = lax.rem(me, 2), lax.div(me, 2)
    pairs = sending.shape[0]
    per = pairs // QUARTERS
    sibling = me + 1 - 2 * core
    order = quarter_order(pair, per)

    loads = [pltpu.make_async_copy(inputs[i], held[i], load_sem.at[i]) for i in range(held_in)]
    for copy in loads:
        copy.start()
    begin()

    loop(1, pairs, lambda s: greet(lax.rem(pair + s, pairs) * 2 + core, cols))
    greet(sibling, cols)
    pl.semaphore_wait(pltpu.get_barrier_semaphore(), pairs)

    def out(e):
        return remote(
            sending.at[e], land.at[pair, core], send.at[e], recv.at[pair], e * 2 + core, cols
        )

    def arrival(e):
        return remote(
            sending.at[e], land.at[e, core], send.at[e], recv.at[e], e * 2 + core, cols
        )

    def share(e):
        block = land.at[e, core]
        return remote(block, block, share_send.at[e], share_recv.at[e], sibling, cols)

    def near(quarter):
        rows = pl.ds(quarter * per, per)
        return remote(
            partial.at[rows, 1 - core],
            inbox.at[rows],
            near_send.at[quarter],
            near_recv.at[quarter],
            sibling,
            cols,
        )

    def back(e):
        return remote(
            inbox.at[e], returned.at[pair], back_send.at[e], back_recv.at[pair], e * 2 + core, cols
        )

    def back_arrival(e):
        return remote(
            inbox.at[e], returned.at[e], back_send.at[e], back_recv.at[e], e * 2 + core, cols
        )

    def others(quarter, action):
        def one(k):
            e = quarter * per + k
            pl.when(e != pair)(lambda: action(e))

        loop(0, per, one)

    own_in = pltpu.make_async_copy(sending.at[pair], land.at[pair, core], own_sem.at[0])
    own_back = pltpu.make_async_copy(inbox.at[pair], returned.at[pair], own_sem.at[1])

    for quarter in (order[2], order[0], order[1], order[3]):
        others(quarter, lambda e: out(e).start())
    own_in.start()
    own_in.wait()
    share(pair).start()
    if work_first:
        run()
    for copy in loads:
        copy.wait()

    def take(quarter):
        def one(e):
            arrival(e).wait_recv()
            share(e).start()

        others(quarter, one)
        loop(0, per, lambda k: share(quarter * per + k).wait_recv())
        step(quarter, per, land, partial, held, scratch)
        near(quarter).start()

    def give(quarter):
        near(quarter).wait_recv()

        def one(k):
            e = quarter * per + k
            inbox[e] = partial[e, core] + inbox[e]
            pl.when(e != pair)(lambda: back(e).start())

        loop(0, per, one)

    take(order[0])
    take(order[1])
    give(order[0])
    give(order[1])
    own_back.start()
    take(order[2])
    give(order[2])
    take(order[3])
    give(order[3])
    if not work_first:
        run()
    final(land, held, scratch, outputs)
    for quarter in order:
        others(quarter, lambda e: out(e).wait_send())
        others(quarter, lambda e: back(e).wait_send())
        others(quarter, lambda e: back_arrival(e).wait_recv())
        loop(0, per, lambda k: share(quarter * per + k).wait_send())
        near(quarter).wait_send()
    own_back.wait()
    end()


def expert_pass(sending, held, out_shape, extra, step, final, work, work_first, cols, collective_id):
    pairs, slots, width = sending.shape
    block = (pairs, slots, width)
    both = (pairs, 2, slots, width)
    sems = pltpu.SemaphoreType.DMA((pairs,))
    scratch = [
        pltpu.VMEM(both, sending.dtype),
        pltpu.VMEM(both, sending.dtype),
        pltpu.VMEM(block, sending.dtype),
    ]
    scratch += [sems] * 8 + [pltpu.SemaphoreType.DMA((2,)), pltpu.SemaphoreType.DMA((len(held),))]
    scratch += [pltpu.VMEM(a.shape, a.dtype) for a in held] + extra + work.scratch()
    out_shape = [jax.ShapeDtypeStruct(block, sending.dtype)] + out_shape
    shapes = (len(held), len(out_shape) - 1, len(extra))
    everywhere = pl.BlockSpec(memory_space=pl.ANY)
    return pl.pallas_call(
        functools.partial(expert_kernel, cols, step, final, work_first, work, shapes),
        out_shape=out_shape + work.out_shape,
        in_specs=[everywhere] * (1 + len(held) + len(work.arrays)),
        out_specs=[everywhere] * (len(out_shape) + len(work.out_shape)),
        scratch_shapes=scratch,
        compiler_params=pltpu.CompilerParams(
            collective_id=collective_id, has_side_effects=True, vmem_limit_bytes=52 * 2**20
        ),
    )(sending, *held, *work.arrays)


def forward_step(quarter, per, land, partial, held, scratch):
    gate, up, down = held
    gate_kept, up_kept, hidden_kept = scratch[:3]
    rows = land[pl.ds(quarter * per, per)].reshape(-1, land.shape[-1])

    def strip(at):
        inner_gate = dot(rows, gate[:, at], (1, 0))
        inner_up = dot(rows, up[:, at], (1, 0))
        gate_kept[quarter, :, at] = inner_gate.astype(jnp.bfloat16)
        up_kept[quarter, :, at] = inner_up.astype(jnp.bfloat16)
        hidden_kept[quarter, :, at] = (apply_silu(inner_gate) * inner_up).astype(jnp.bfloat16)

    strips(gate.shape[1], strip)
    total = dot(hidden_kept[quarter], down[...], (1, 0)).astype(jnp.bfloat16)
    partial[pl.ds(quarter * per, per)] = total.reshape((per,) + partial.shape[1:])


def forward_final(land, held, scratch, outputs):
    sems = scratch[3]
    copies = [
        pltpu.make_async_copy(source, outputs[i], sems.at[i])
        for i, source in enumerate((land,) + tuple(scratch[:3]))
    ]
    for copy in copies:
        copy.start()
    for copy in copies:
        copy.wait()


def expert_forward(sending, gate, up, down, work, cols, collective_id):
    pairs, slots, width = sending.shape
    kept = (QUARTERS, 2 * pairs * slots // QUARTERS, gate.shape[1])
    out_shape = [jax.ShapeDtypeStruct((pairs, 2, slots, width), sending.dtype)]
    out_shape += [jax.ShapeDtypeStruct(kept, sending.dtype)] * 3
    extra = [pltpu.VMEM(kept, sending.dtype)] * 3 + [pltpu.SemaphoreType.DMA((4,))]
    return expert_pass(
        sending, [gate, up, down], out_shape, extra, forward_step, forward_final, work, False,
        cols, collective_id,
    )


def backward_step(quarter, per, land, partial, held, scratch):
    gate, up, down, _, gate_kept, up_kept, _ = held
    grads = land[pl.ds(quarter * per, per)].reshape(-1, land.shape[-1])

    def strip(at):
        upstream = dot(grads, down[at, :], (1, 1))
        inner_gate = gate_kept[quarter, :, at].astype(jnp.float32)
        inner_up = up_kept[quarter, :, at].astype(jnp.float32)
        gate_kept[quarter, :, at] = (upstream * inner_up * silu_slope(inner_gate)).astype(
            jnp.bfloat16
        )
        up_kept[quarter, :, at] = (upstream * apply_silu(inner_gate)).astype(jnp.bfloat16)

    strips(gate.shape[1], strip)
    total = dot(gate_kept[quarter], gate[...], (1, 1)) + dot(up_kept[quarter], up[...], (1, 1))
    partial[pl.ds(quarter * per, per)] = total.astype(jnp.bfloat16).reshape(
        (per,) + partial.shape[1:]
    )


GRAD_STRIP = 256


def backward_final(land, held, scratch, outputs):
    _, _, _, rows, low_gate, low_up, hidden = held
    buffers, sems = scratch
    width, inner = land.shape[-1], hidden.shape[-1]
    row_count = low_gate.shape[0] * low_gate.shape[1]
    started = {}

    def flat(ref):
        return ref[...].reshape(row_count, ref.shape[-1])

    def turned(ref, at):
        lead = ref.shape[:-1]
        return ref[(slice(None),) * len(lead) + (at,)].reshape(row_count, GRAD_STRIP).T

    def store(slot, part, value, target):
        if (slot, part) in started:
            started[slot, part].wait()
        view = buffers.at[slot, part, :, pl.ds(0, value.shape[1])]
        buffers[slot, part, :, 0 : value.shape[1]] = value
        copy = pltpu.make_async_copy(view, target, sems.at[slot, part])
        copy.start()
        started[slot, part] = copy

    for j in range(width // GRAD_STRIP):
        at = slice(j * GRAD_STRIP, (j + 1) * GRAD_STRIP)
        left = turned(rows, at)
        store(j % 2, 0, dot(left, flat(low_gate), (1, 0)), outputs[0].at[at])
        store(j % 2, 1, dot(left, flat(low_up), (1, 0)), outputs[1].at[at])
    for j in range(inner // GRAD_STRIP):
        at = slice(j * GRAD_STRIP, (j + 1) * GRAD_STRIP)
        value = dot(turned(hidden, at), land[...].reshape(row_count, width), (1, 0))
        store(j % 2, j // 2 % 2, value, outputs[2].at[at])
    for copy in started.values():
        copy.wait()


def expert_backward(sending, gate, up, down, kept, work, cols, collective_id):
    out_shape = [jax.ShapeDtypeStruct(w.shape, jnp.float32) for w in (gate, up, down)]
    widest = max(gate.shape[1], down.shape[1])
    extra = [
        pltpu.VMEM((2, 2, GRAD_STRIP, widest), jnp.float32),
        pltpu.SemaphoreType.DMA((2, 2)),
    ]
    return expert_pass(
        sending, [gate, up, down] + list(kept), out_shape, extra, backward_step, backward_final,
        work, True, cols, collective_id,
    )


def on_device(
    hidden_in,
    w_query,
    w_key,
    w_value,
    w_out,
    norm_attn,
    norm_ffn,
    w_router,
    shared_gate,
    shared_up,
    shared_down,
    expert_gate,
    expert_up,
    expert_down,
    teacher,
    routes,
    cont_lengths,
    valid_mask,
):
    rows_dev, groups, model_width = hidden_in.shape
    tokens = rows_dev * groups
    head_count = lax.axis_size("head")
    cols = lax.axis_size("blk")
    devices = head_count * cols
    slices = devices // EXPERTS
    pairs = devices // 2
    shard = w_query.shape[0]
    hidden = shared_gate.shape[1]
    bf16, f32 = jnp.bfloat16, jnp.float32
    me = flat_index(cols)
    core, pair = lax.rem(me, 2), lax.div(me, 2)
    holds, unit = unit_place(pair)

    packed = jnp.concatenate([w_query, w_key, w_value], axis=1)
    router_size = shard * EXPERTS
    router_rows = -(-router_size // 128)
    router_pad = router_rows * 128 - router_size

    def in_rows(gains_first, gains_second, scalar, router):
        count = gains_first.shape[0]
        pieces = [
            jnp.pad(gains_first.astype(f32), ((0, 0), (0, 128 - shard))),
            jnp.pad(gains_second.astype(f32), ((0, 0), (0, 128 - shard))),
            jnp.broadcast_to(scalar, (count, 128)),
            jnp.pad(router.astype(f32), ((0, 0), (0, router_pad + (5 - router_rows) * 128))),
        ]
        return jnp.concatenate(pieces, axis=1).reshape(count, 8, 128)

    small = in_rows(
        norm_attn[None],
        norm_ffn[None],
        jnp.sum(valid_mask.astype(f32)),
        w_router.reshape(1, router_size),
    )[0]
    all_packed, all_small = gather_all([packed, small], cols, 0)
    proj_mat = all_packed.reshape(model_width, 3 * model_width)
    all_small = all_small.reshape(devices, 8, 128)
    gain_attn = all_small[:, 0, :shard].reshape(model_width)
    gain_ffn = all_small[:, 1, :shard].reshape(model_width)
    valid_total = jnp.sum(all_small[:, 2, 0])
    route_mat = (
        all_small[:, 3 : 3 + router_rows]
        .reshape(devices, router_rows * 128)[:, :router_size]
        .reshape(model_width, EXPERTS)
        .astype(bf16)
    )

    wide = jnp.concatenate([shared_gate, shared_up], axis=1)
    share_wide = lax.all_gather(wide, AXES, axis=0, tiled=True)

    local_pos = me * rows_dev + jnp.arange(rows_dev, dtype=jnp.int32)
    local_begin = segment_starts(local_pos, cont_lengths)
    cosine, sine = rotary_tables(local_pos, local_begin)
    flat_in = hidden_in.reshape(tokens, model_width)
    def rotated(halves, sine_now):
        first, second = halves[:, 0], halves[:, 1]
        return jnp.concatenate(
            [first * cosine - second * sine_now, second * cosine + first * sine_now], axis=1
        )

    def by_unit(blocks):
        rows = blocks.shape[1]
        return (
            blocks.reshape(HEADS, rows, rows_dev, groups)
            .transpose(3, 0, 1, 2)
            .reshape(groups * HEADS, rows, rows_dev)
        )

    def by_head(blocks):
        rows = blocks.shape[1]
        return (
            blocks.reshape(groups, HEADS, rows, rows_dev)
            .transpose(1, 2, 3, 0)
            .reshape(HEADS, rows, tokens)
        )

    at_home = rows_dev == TILE and groups == 1
    if at_home:
        normed_attn, scaling_attn, q_blocks, kv_blocks = project(
            flat_in, gain_attn, proj_mat, cosine, sine, cols, 1
        )
    else:
        normed_exact, scaling_attn = root_norm(flat_in, gain_attn)
        normed_attn = normed_exact.astype(bf16)
        projected = dot(proj_mat, normed_attn, (0, 1)).reshape(
            3, HEADS, 2, HEAD_DIM // 2, tokens
        )
        qkv_blocks = jnp.concatenate(
            [
                rotated(projected[0], sine),
                rotated(projected[1], sine),
                projected[2].reshape(HEADS, HEAD_DIM, tokens),
            ],
            axis=1,
        ).astype(bf16)
        q_blocks, kv_blocks = to_units(by_unit(qkv_blocks), cols, True, 1)

    unit_lengths = lax.dynamic_slice_in_dim(
        cont_lengths, jnp.minimum(unit // HEADS, groups - 1), 1, axis=0
    )
    place = (
        (2 * jnp.arange(pairs, dtype=jnp.int32) + core)[:, None] * rows_dev
        + jnp.arange(rows_dev, dtype=jnp.int32)
    ).reshape(-1)
    run = segment_starts(place, unit_lengths).reshape(-1, 1, TILE)
    queries, keys_values = to_tiles(q_blocks), to_tiles(kv_blocks)
    if at_home:
        exact, lse, attended, out_mat, share_down = attend_home(
            queries, keys_values, run, [w_out, shared_down], cols, 2
        )
    else:
        exact, low, lse = attend(queries, keys_values, run, rows_dev)
        (attended,) = to_tokens([from_tiles(low, rows_dev)], cols, 2)
        out_mat, share_down = gather_all([w_out, shared_down], cols, 11)
    out_mat = out_mat.reshape(model_width, model_width)
    share_down = share_down.reshape(hidden, model_width)
    attended = by_head(attended).reshape(model_width, tokens)

    residual_mid = flat_in + dot(attended, out_mat, (0, 0))
    normed_mid, scaling_ffn = root_norm(residual_mid, gain_ffn)
    normed_ffn = normed_mid.astype(bf16)

    route_flat = routes.reshape(tokens, TOP)
    route_onehot = (route_flat[:, :, None] == jnp.arange(EXPERTS, dtype=jnp.int32)).astype(f32)
    flat_routes = route_flat.reshape(-1)
    route_hits = (flat_routes[:, None] == jnp.arange(EXPERTS, dtype=jnp.int32)).astype(bf16)
    order = jnp.arange(tokens * TOP, dtype=jnp.int32)
    before = dot((order[None, :] < order[:, None]).astype(bf16), route_hits, (1, 0))
    ranking = jnp.sum(before * route_hits.astype(f32), axis=1).astype(jnp.int32)
    slot_of = (flat_routes * CAP + ranking).reshape(tokens, TOP)
    slot_ids = jnp.arange(EXPERTS * CAP, dtype=jnp.int32)
    place_first = (slot_ids[:, None] == slot_of[None, :, 0]).astype(bf16)
    place_second = (slot_ids[:, None] == slot_of[None, :, 1]).astype(bf16)

    sending = dot(place_first + place_second, normed_ffn, (1, 0)).astype(bf16)
    sending = sending.reshape(EXPERTS, CAP, model_width)

    logits = dot(normed_ffn, route_mat, (1, 0))
    chosen = jnp.sum(route_onehot * logits[:, None, :], axis=-1)
    gate_probs = jax.nn.softmax(chosen, axis=1)
    out = jax.ShapeDtypeStruct
    shared_work = Work(
        [normed_ffn, share_wide, share_down],
        [
            out((tokens, hidden), bf16),
            out((tokens, hidden), bf16),
            out((tokens, hidden), bf16),
            out((tokens, model_width), f32),
        ],
        shared_forward,
    )
    if slices == 2:
        passed = expert_forward(
            sending, expert_gate, expert_up, expert_down, shared_work, cols, 3
        )
        returned, kept, shared_results = passed[0], passed[1:5], passed[5:]
    else:
        (arrived,) = spread([sending], cols, slices, EXPERTS, 3)
        arrived = arrived.reshape(devices * CAP, model_width)
        inner_gate = dot(arrived, expert_gate, (1, 0))
        inner_up = dot(arrived, expert_up, (1, 0))
        inner_hidden = (apply_silu(inner_gate) * inner_up).astype(bf16)
        partial_out = dot(inner_hidden, expert_down, (1, 0)).astype(bf16)
        returned, *shared_results = collect(
            [partial_out.reshape(slices, EXPERTS, CAP, model_width)], cols, 4, shared_work
        )
    shared_gate_in, shared_up_in, shared_hidden, shared_out = shared_results
    expert_rows = returned.reshape(EXPERTS * CAP, model_width)
    routed_first = dot(place_first, expert_rows, (0, 0))
    routed_second = dot(place_second, expert_rows, (0, 0))
    mixture = gate_probs[:, 0:1] * routed_first + gate_probs[:, 1:2] * routed_second
    layer_flat = residual_mid + shared_out + mixture

    keep_rows = valid_mask.reshape(tokens).astype(f32)[:, None]
    deviation = layer_flat - teacher.reshape(tokens, model_width)
    loss_local = jnp.sum(keep_rows * deviation * deviation)
    grad_rows = keep_rows * deviation * (tokens * devices / valid_total)
    back_first = (gate_probs[:, 0:1] * grad_rows).astype(bf16)
    back_second = (gate_probs[:, 1:2] * grad_rows).astype(bf16)
    back_send = (
        dot(place_first, back_first, (1, 0)) + dot(place_second, back_second, (1, 0))
    ).astype(bf16)
    shared_work = Work(
        [
            grad_rows.astype(bf16),
            normed_ffn,
            shared_gate_in,
            shared_up_in,
            shared_hidden,
            share_wide,
            share_down,
        ],
        [
            out(share_wide.shape, bf16),
            out(share_down.shape, bf16),
            out((tokens, model_width), f32),
        ],
        shared_backward,
        {0: 5, 1: 6},
    )
    back_send = back_send.reshape(EXPERTS, CAP, model_width)
    if slices == 2:
        passed = expert_backward(
            back_send, expert_gate, expert_up, expert_down, kept, shared_work, cols, 5
        )
        back_returned, grad_expert_gate, grad_expert_up, grad_expert_down = passed[:4]
        grad_share_wide, grad_share_down, shared_back = passed[4:]
    else:
        back_arrived, grad_share_wide, grad_share_down, shared_back = spread(
            [back_send], cols, slices, EXPERTS, 5, shared_work
        )
        back_arrived = back_arrived.reshape(devices * CAP, model_width)
        grad_inner = dot(back_arrived, expert_down, (1, 1))
        grad_inner_gate = (grad_inner * inner_up * silu_slope(inner_gate)).astype(bf16)
        grad_inner_up = (grad_inner * apply_silu(inner_gate)).astype(bf16)
        back_partial = (
            dot(grad_inner_gate, expert_gate, (1, 1)) + dot(grad_inner_up, expert_up, (1, 1))
        ).astype(bf16)
        (back_returned,) = collect(
            [back_partial.reshape(slices, EXPERTS, CAP, model_width)], cols, 6
        )
        grad_expert_down = dot(inner_hidden, back_arrived, (0, 0))
        grad_expert_gate = dot(arrived, grad_inner_gate, (0, 0))
        grad_expert_up = dot(arrived, grad_inner_up, (0, 0))

    grad_gate = jnp.stack(
        [jnp.sum(grad_rows * routed_first, axis=-1), jnp.sum(grad_rows * routed_second, axis=-1)],
        axis=1,
    )
    grad_chosen = gate_probs * (grad_gate - jnp.sum(gate_probs * grad_gate, axis=1, keepdims=True))
    grad_logits = jnp.sum(route_onehot * grad_chosen[:, :, None], axis=1).astype(bf16)
    grad_route_mat = dot(normed_ffn, grad_logits, (0, 0))

    back_rows = back_returned.reshape(EXPERTS * CAP, model_width)
    grad_normed = (
        dot(place_first + place_second, back_rows, (0, 0))
        + dot(grad_logits, route_mat, (1, 1))
        + shared_back
    )

    grad_mid_norm, grad_gain_ffn = root_norm_back(residual_mid, scaling_ffn, gain_ffn, grad_normed)
    grad_mid = grad_rows + grad_mid_norm
    grad_mid_low = grad_mid.astype(bf16)
    grad_attended = dot(out_mat, grad_mid_low, (1, 1)).astype(bf16)
    grad_out_mat = dot(attended, grad_mid_low, (1, 0))
    grad_blocks = by_unit(grad_attended.reshape(HEADS, HEAD_DIM, tokens))
    spots = (2, cols // 4, 2, 2)
    parts = [
        grad_share_wide.reshape(spots + (shard, 2 * hidden)),
        grad_share_down.reshape(spots + shared_down.shape),
        grad_out_mat.astype(bf16).reshape(spots + (shard, model_width)),
    ]
    if at_home:
        dq, dkv, share_sums, grad_share_down, grad_out_sum = attend_back_home(
            queries, keys_values, grad_blocks, exact, lse, run, parts, cols, 10
        )
    else:
        (grad_blocks,) = to_units(grad_blocks, cols, False, 7)
        dq, dkv, share_sums, grad_share_down, grad_out_sum = attend_back(
            queries, keys_values, to_tiles(grad_blocks), exact, lse, run, rows_dev, parts, cols, 10
        )
        dq, dkv = to_tokens([from_tiles(dq, rows_dev), from_tiles(dkv, rows_dev)], cols, 8)
    dq, dkv = by_head(dq).astype(f32), by_head(dkv)

    def halves_of(rows):
        return rows.reshape(HEADS, 2, HEAD_DIM // 2, tokens)

    grad_proj = jnp.concatenate(
        [
            rotated(halves_of(dq), -sine).astype(bf16).reshape(model_width, tokens),
            rotated(halves_of(dkv[:, :HEAD_DIM].astype(f32)), -sine)
            .astype(bf16)
            .reshape(model_width, tokens),
            dkv[:, HEAD_DIM:].reshape(model_width, tokens),
        ],
        axis=0,
    )
    grad_normed_attn = dot(grad_proj, proj_mat, (0, 1))
    grad_in_norm, grad_gain_attn = root_norm_back(
        flat_in, scaling_attn, gain_attn, grad_normed_attn
    )
    input_grad = (grad_mid + grad_in_norm).reshape(rows_dev, groups, model_width)

    grad_attn = dot(normed_attn, grad_proj, (0, 1)).astype(bf16)
    tail = in_rows(
        grad_gain_attn.reshape(devices, shard),
        grad_gain_ffn.reshape(devices, shard),
        loss_local,
        grad_route_mat.reshape(devices, router_size),
    )
    attn_sums, tail_sums = reduce_all(
        [grad_attn.reshape(spots + (shard, 3 * model_width)), tail.reshape(spots + (8, 128))],
        cols,
        9,
    )
    loss_value = tail_sums[2, 0] / (valid_total * model_width)
    return (
        layer_flat.reshape(rows_dev, groups, model_width),
        input_grad,
        loss_value,
        attn_sums[:, :model_width],
        attn_sums[:, model_width : 2 * model_width],
        attn_sums[:, 2 * model_width :],
        grad_out_sum,
        tail_sums[0, :shard],
        tail_sums[1, :shard],
        tail_sums[3 : 3 + router_rows].reshape(-1)[:router_size].reshape(shard, EXPERTS),
        share_sums[:, :hidden],
        share_sums[:, hidden:],
        grad_share_down,
        grad_expert_gate,
        grad_expert_up,
        grad_expert_down,
    )


def solution(mesh):
    placed = (
        P(("head", "blk"), None, None),
        P(("head", "blk"), None),
        P(("head", "blk"), None),
        P(("head", "blk"), None),
        P(("head", "blk"), None),
        P(("head", "blk")),
        P(("head", "blk")),
        P(("head", "blk"), None),
        P(("head", "blk"), None),
        P(("head", "blk"), None),
        P(("head", "blk"), None),
        P(None, ("head", "blk")),
        P(None, ("head", "blk")),
        P(("head", "blk"), None),
        P(("head", "blk"), None, None),
        P(("head", "blk"), None, None),
        P(),
        P(("head", "blk"), None),
    )
    return jax.shard_map(
        on_device,
        mesh=mesh,
        in_specs=placed,
        out_specs=(
            P(("head", "blk"), None, None),
            P(("head", "blk"), None, None),
            P(),
            P(("head", "blk"), None),
            P(("head", "blk"), None),
            P(("head", "blk"), None),
            P(("head", "blk"), None),
            P(("head", "blk")),
            P(("head", "blk")),
            P(("head", "blk"), None),
            P(("head", "blk"), None),
            P(("head", "blk"), None),
            P(("head", "blk"), None),
            P(None, ("head", "blk")),
            P(None, ("head", "blk")),
            P(("head", "blk"), None),
        ),
        check_vma=False,
    )
```

time: 1810 us -> 507 us (0.28)
  waiting for transfers between devices: 918 us -> 0.02 us
  Pallas kernels: 0 us -> 423 us
  matrix products: 389 us -> 20.1 us
  blocking collectives: 304 us -> 0 us
  other arithmetic: 81.5 us -> 11.1 us
  local copies, waits for them, and re-layouts: 74.3 us -> 30.2 us
  starting transfers between devices: 20.3 us -> 0.04 us
    reduce_scatter x7 -> x0, waiting for transfers between devices: 496 us -> none  [the longest x1 105 us: on_device(): lax.psum_scatter(grad_out_mat, ('head', 'blk'), scatter_dimension=0, tile...]
    pallas_call x0 -> x7, Pallas kernels: none -> 423 us  [the longest x2 154 us: expert_pass(): pl.pallas_call(functools.partial(expert_kernel, cols, step, final, work_f...]
    dot_general x42 -> x15, matrix products: 389 us -> 20.1 us  [dot(): lax.dot_general(left, right, (((over[0],), (over[1],)), ((), ())), prefer...]
    all_to_all x5 -> x0, waiting for transfers between devices: 265 us -> none  [the longest x2 196 us: to_experts(): lax.all_to_all(buffer_rows, ('head', 'blk'), split_axis=0, concat_axis=0,...]
    all_gather x11 -> x1, waiting for transfers between devices: 152 us -> 0.01 us  [on_device(): share_wide = lax.all_gather(wide, AXES, axis=0, tiled=True)]
    psum x2 -> x0, blocking collectives: 144 us -> none  [the longest x1 105 us: on_device(): lax.psum(jnp.sum(valid_mask.astype(jnp.float32)), ('head', 'blk'))]
    all_gather x2 -> x0, blocking collectives: 60.2 us -> none  [the longest x1 41.2 us: on_device(): lax.all_gather(w_router, ('head', 'blk'), axis=0, tiled=True)]
    all_to_all x3 -> x0, blocking collectives: 57.2 us -> none  [the longest x1 28.9 us: from_heads(): lax.all_to_all(stacked, 'head', split_axis=1, concat_axis=3, tiled=True)]
  transfers between devices with their start and end apart: 23 -> 1, of which waited for: 13 -> 0; matrix products, arithmetic and copies ran while one was open for 29% -> 3% of each run, Pallas kernels for 0% -> 26%
where the time goes in v1:
time: 507 us; the launch traced here: 503 us
  Pallas kernels  423 us (83%)
  local copies, waits for them, and re-layouts  30.2 us (6%)
  matrix products  20.1 us (4%)
  between operations  18.3 us (4%)
  other arithmetic  11.1 us (2%)
    pallas_call x2, Pallas kernels, expert_pass(): pl.pallas_call(functools.partial(expert_kernel, cols, step, final, work_f...  154 us
    pallas_call x1, Pallas kernels, attend_back_home(): pl.pallas_call(functools.partial(backward_home_kernel, cols, depths, len(...  111 us
    pallas_call x1, Pallas kernels, attend_home(): pl.pallas_call(functools.partial(forward_home_kernel, cols, len(shards)),...  67.7 us
    pallas_call x1, Pallas kernels, project(): pl.pallas_call(functools.partial(project_kernel, cols), out_shape=[jax.Sh...  31.1 us
    pallas_call x1, Pallas kernels, gather_all(): pl.pallas_call(functools.partial(gather_kernel, depths, count), out_shape...  30.3 us
    pallas_call x1, Pallas kernels, reduce_all(): pl.pallas_call(functools.partial(reduce_kernel, depths, count), out_shape...  29.9 us
    unnamed x69, local copies, waits for them, and re-layouts  21.8 us
    dot_general x15, matrix products, dot(): lax.dot_general(left, right, (((over[0],), (over[1],)), ((), ())), prefer...  20.1 us
  transfers between devices with their start and end apart: 1, of which 0 were waited for; matrix products, arithmetic and copies ran while one was open for 3% of the time, Pallas kernels for 26%

profile of v1, /device:TPU:0, one launch (start us, length us, event | category | flops | bytes accessed | tf_op | source)
XLA Modules:
  0.0 503.1 jit_solution(17430976272111201591)
XLA Ops:
  7.2 1.7 pad_maximum_fusion.5
  15.2 30.3 %shard_map.297 = (bf16[2,4,2,2,24,2304]{5,4,3,2,1,0:T(8,128)(2,1)}, f32[2,4,2,2,8,128]{5,4,3,2,1,0:T(8,128)}) custom-call(bf16[24,2304]{1,0:T(8,128)(2,1)} %pad_maximum_fusion.6.refs_0_, f32[8,128]{1,0:T(8,128)} %bitcast.158), custom_call_target="tpu_custom_call" | custom-call | tf_op jit(solution)/shard_map/pallas_call | solution.py:517
  50.2 1.5 slice_reduce_fusion.2
  53.7 2.0 copy-done.3
  55.7 31.1 %shard_map.298 = (bf16[256,768]{1,0:T(8,128)(2,1)S(1)}, f32[256,1]{1,0:T(8,128)S(1)}, bf16[16,64,256]{2,1,0:T(8,128)(2,1)S(1)}, bf16[32,128,256]{2,1,0:T(8,128)(2,1)S(1)}) custom-call(f32[256,768]{1,0:T(8,128)S(1)} %bitcast.125, f32[1,768]{1,0:T(1,128)S(1)} %reshape_reshape_squeeze.3.gain_ref, bf16[768,2304]{1,0:T(8,128)(2,1)S(1)} %bitcast.123, ...), custom_call_target="tpu_custom_call" | custom-call | tf_op jit(solution)/shard_map/pallas_call | solution.py:989
  87.7 67.7 %shard_map.299 = (f32[16,64,256]{2,1,0:T(8,128)S(1)}, f32[16,1,256]{2,1,0:T(1,128)S(1)}, bf16[12,64,256]{2,1,0:T(8,128)(2,1)S(1)}, bf16[2,4,2,2,24,768]{5,4,3,2,...) custom-call(bf16[16,64,256]{2,1,0:T(8,128)(2,1)S(1)} %get-tuple-element.52.refs_0_, ...), custom_call_target="tpu_custom_call" | custom-call | tf_op jit(solution)/shard_map/pallas_call | solution.py:1365
  158.0 1.8 convolution_convert_fusion.1
  159.7 74.3 %shard_map.300 = (bf16[16,64,768]{2,1,0:T(8,128)(2,1)}, bf16[16,2,64,768]{3,2,1,0:T(8,128)(2,1)}, bf16[4,512,1024]{2,1,0:T(8,128)(2,1)}, bf16[4,512,1024]{2,1,0:...) custom-call(bf16[16,64,768]{2,1,0:T(8,128)(2,1)} %bitcast.145, ...), custom_call_target="tpu_custom_call" | custom-call | tf_op jit(solution)/shard_map/pallas_call | solution.py:1918
  234.1 2.2 fusion.5
  236.3 2.8 fusion.7
  241.1 1.8 add_convert_fusion
  242.9 79.4 %shard_map.301 = (bf16[16,64,768]{2,1,0:T(8,128)(2,1)}, f32[768,1024]{1,0:T(8,128)}, f32[768,1024]{1,0:T(8,128)}, f32[1024,768]{1,0:T(8,128)}, bf16[768,4096]{1,...) custom-call(bf16[16,64,768]{2,1,0:T(8,128)(2,1)} %bitcast.136, bf16[768,1024]{1,0:T(8,128)(2,1)} %refs_1_.3, ...), custom_call_target="tpu_custom_call" | custom-call | tf_op jit(solution)/shard_map/pallas_call | solution.py:1918
  322.3 2.1 fusion.9
  326.6 1.5 convolution_convert_fusion.2
  329.1 110.6 %shard_map.302 = (bf16[12,64,256]{2,1,0:T(8,128)(2,1)S(1)}, bf16[12,128,256]{2,1,0:T(8,128)(2,1)}, f32[24,4096]{1,0:T(8,128)S(1)}, f32[64,768]{1,0:T(8,128)S(1)}, f32[24,768]{1,0:T(8,128)S(1)}) custom-call(bf16[16,64,256]{2,1,0:T(8,128)(2,1)S(1)} %copy-done.6, bf16[32,128,256]{2,1,0:T(8,128)(2,1)} %copy-done, f32[16,64,256]{2,1,0:T(8,128)} %copy-done.7, ...), custom_call_target="tpu_custom_call" | custom-call | tf_op jit(solution)/shard_map/pallas_call | solution.py:1650
  441.3 1.6 copy-done.4
  443.1 2.1 multiply_reduce_fusion.1
  445.3 2.9 convolution_convert_fusion
  448.2 29.9 %shard_map.303 = (f32[24,2304]{1,0:T(8,128)S(1)}, f32[8,128]{1,0:T(8,128)S(1)}) custom-call(bf16[2,4,2,2,24,2304]{5,4,3,2,1,0:T(8,128)(2,1)} %bitcast.139, f32[2,4,2,2,8,128]{5,4,3,2,1,0:T(8,128)S(1)} %bitcast.129), custom_call_target="tpu_custom_call" | custom-call | tf_op jit(solution)/shard_map/pallas_call | solution.py:719
  479.1 1.7 copy.78
  481.9 1.7 copy.79
  487.0 1.7 copy.113
  490.0 1.7 copy.114
  493.0 1.7 copy.115
  (138 shorter events, 29.2 us)
Async XLA Ops:
  7.2 46.2 %copy-start.27 = (s32[1,8]{1,0:T(1,128)S(1)}, s32[1,8]{1,0:T(1,128)}, u32[]{:S(2)}) copy-start(s32[1,8]{1,0:T(1,128)} %param.34) | copy-start | bytes 100
  7.2 42.9 %copy-start.16 = (f32[256,1,768]{2,1,0:T(1,128)S(1)}, f32[256,1,768]{2,1,0:T(1,128)}, u32[]{:S(2)}) copy-start(f32[256,1,768]{2,1,0:T(1,128)} %param.18) | copy-start | bytes 2359300
  7.2 152.5 %all-gather.2.cloned.1.call-start = ((), (), s32[]{:S(2)}) async-start(), calls=%async_computation | async-start | bytes 6488064 | tf_op jit(solution)/shard_map/all_gather | solution.py:2112
  53.2 34.5 %copy-start.8 = (bf16[64,768]{1,0:T(8,128)(2,1)S(1)}, bf16[64,768]{1,0:T(8,128)(2,1)}, u32[]{:S(2)}) copy-start(bf16[64,768]{1,0:T(8,128)(2,1)} %refs_4_.1) | copy-start | bytes 294916
  53.2 34.5 %copy-start.9 = (bf16[24,768]{1,0:T(8,128)(2,1)S(1)}, bf16[24,768]{1,0:T(8,128)(2,1)}, u32[]{:S(2)}) copy-start(bf16[24,768]{1,0:T(8,128)(2,1)} %refs_3_.3) | copy-start | bytes 110596
  53.7 2.0 copy-start.3
  87.6 68.5 %copy-start = (bf16[32,128,256]{2,1,0:T(8,128)(2,1)}, bf16[32,128,256]{2,1,0:T(8,128)(2,1)S(1)}, u32[]{:S(2)}) copy-start(bf16[32,128,256]{2,1,0:T(8,128)(2,1)S(1)} %get-tuple-element.53.refs_1_) | copy-start | bytes 6291460
  87.6 68.5 %copy-start.5 = (bf16[16,64,256]{2,1,0:T(8,128)(2,1)}, bf16[16,64,256]{2,1,0:T(8,128)(2,1)S(1)}, u32[]{:S(2)}) copy-start(bf16[16,64,256]{2,1,0:T(8,128)(2,1)S(1)} %get-tuple-element.52.refs_0_) | copy-start | bytes 1572868
  87.6 67.9 %copy-start.17 = (f32[256,1,768]{2,1,0:T(1,128)S(1)}, f32[256,1,768]{2,1,0:T(1,128)}, u32[]{:S(2)}) copy-start(f32[256,1,768]{2,1,0:T(1,128)} %param.18) | copy-start | bytes 2359300
  155.5 1.9 copy-start.1
  234.1 2.2 copy-start.13
  234.1 2.2 copy-start.25
  326.1 2.0 copy-start.14
  326.1 2.9 copy-start.6
  440.9 2.0 copy-start.4
  440.9 2.2 copy-start.18
  443.1 2.2 copy-start.11
  448.2 30.9 %copy-start.21 = (f32[256,768]{1,0:T(8,128)S(1)}, f32[256,768]{1,0:T(8,128)}, u32[]{:S(2)}) copy-start(f32[256,768]{1,0:T(8,128)} %copy-done.20) | copy-start | bytes 2359300
  448.2 33.4 %copy-start.15 = (f32[256,768]{1,0:T(8,128)S(1)}, f32[256,768]{1,0:T(8,128)}, u32[]{:S(2)}) copy-start(f32[256,768]{1,0:T(8,128)} %copy-done.14) | copy-start | bytes 2359300
  448.2 33.4 %copy-start.19 = (f32[256,1,768]{2,1,0:T(1,128)S(1)}, f32[256,1,768]{2,1,0:T(1,128)}, u32[]{:S(2)}) copy-start(f32[256,1,768]{2,1,0:T(1,128)} %param.18) | copy-start | bytes 2359300
  448.2 33.4 %copy-start.26 = (f32[256,768]{1,0:T(8,128)S(1)}, f32[256,768]{1,0:T(8,128)}, u32[]{:S(2)}) copy-start(f32[256,768]{1,0:T(8,128)} %get-tuple-element.189) | copy-start | bytes 2359300
  481.6 5.4 %copy-start.24 = (f32[768,1024]{1,0:T(8,128)S(1)}, f32[768,1024]{1,0:T(8,128)}, u32[]{:S(2)}) copy-start(f32[768,1024]{1,0:T(8,128)} %get-tuple-element.221) | copy-start | bytes 9437188
  487.0 3.0 copy-start.23
  490.0 3.0 copy-start.22
  (5 other events, 5.8 us)
Sparse Core Ops, SparseCore 0:
  11.5 93.9 all-gather.1

commit v2 on v1

--- a/solution.py
+++ b/solution.py
@@ -52,8 +52,9 @@
 
 
 def segment_starts(positions, cont_lengths):
-    run_ends = jnp.cumsum(cont_lengths, axis=1)
-    begins = PROMPT + run_ends - cont_lengths
+    count = cont_lengths.shape[1]
+    earlier = jnp.arange(count)[None, :] < jnp.arange(count)[:, None]
+    begins = PROMPT + jnp.sum(jnp.where(earlier, cont_lengths[:, None, :], 0), axis=2)
     passed = begins[None, :, :] <= positions[:, None, None]
     return jnp.max(jnp.where(passed, begins[None], 0), axis=-1)
 
@@ -1285,7 +1286,7 @@
     ]
 
 
-GATHER_AT = {"start": 0, "start_own": 0, "spread_near": 7, "spread_far": 10, "settle": 13}
+GATHER_AT = {"start": 0, "start_own": 0, "spread_near": 8, "spread_far": 11, "settle": 14}
 
 
 def forward_home_kernel(cols, count, *refs):
@@ -2109,7 +2110,6 @@
     )
 
     wide = jnp.concatenate([shared_gate, shared_up], axis=1)
-    share_wide = lax.all_gather(wide, AXES, axis=0, tiled=True)
 
     local_pos = me * rows_dev + jnp.arange(rows_dev, dtype=jnp.int32)
     local_begin = segment_starts(local_pos, cont_lengths)
@@ -2168,15 +2168,16 @@
     run = segment_starts(place, unit_lengths).reshape(-1, 1, TILE)
     queries, keys_values = to_tiles(q_blocks), to_tiles(kv_blocks)
     if at_home:
-        exact, lse, attended, out_mat, share_down = attend_home(
-            queries, keys_values, run, [w_out, shared_down], cols, 2
+        exact, lse, attended, out_mat, share_down, share_wide = attend_home(
+            queries, keys_values, run, [w_out, shared_down, wide], cols, 2
         )
     else:
         exact, low, lse = attend(queries, keys_values, run, rows_dev)
         (attended,) = to_tokens([from_tiles(low, rows_dev)], cols, 2)
-        out_mat, share_down = gather_all([w_out, shared_down], cols, 11)
+        out_mat, share_down, share_wide = gather_all([w_out, shared_down, wide], cols, 11)
     out_mat = out_mat.reshape(model_width, model_width)
     share_down = share_down.reshape(hidden, model_width)
+    share_wide = share_wide.reshape(model_width, 2 * hidden)
     attended = by_head(attended).reshape(model_width, tokens)
 
     residual_mid = flat_in + dot(attended, out_mat, (0, 0))

time: 507 us -> 499 us (0.984)
  between operations: 18.3 us -> 4.63 us
  Pallas kernels: 423 us -> 429 us
    pallas_call x1, Pallas kernels: 67.7 us -> 78.5 us  [attend_home(): pl.pallas_call(functools.partial(forward_home_kernel, cols, len(shards)),...]
    pallas_call x1, Pallas kernels: 31.1 us -> 25.5 us  [project(): pl.pallas_call(functools.partial(project_kernel, cols), out_shape=[jax.Sh...]
    unnamed x69 -> x55, local copies, waits for them, and re-layouts: 21.8 us -> 22.8 us
  transfers between devices with their start and end apart: 1 -> 0, of which waited for: 0 -> 0; matrix products, arithmetic and copies ran while one was open for 3% -> 0% of each run, Pallas kernels for 26% -> 0%
where the time goes in v2:
time: 499 us; the launch traced here: 495 us
  Pallas kernels  429 us (86%)
  local copies, waits for them, and re-layouts  30.1 us (6%)
  matrix products  20.4 us (4%)
  other arithmetic  10.4 us (2%)
    pallas_call x2, Pallas kernels, expert_pass(): pl.pallas_call(functools.partial(expert_kernel, cols, step, final, work_f...  154 us
    pallas_call x1, Pallas kernels, attend_back_home(): pl.pallas_call(functools.partial(backward_home_kernel, cols, depths, len(...  112 us
    pallas_call x1, Pallas kernels, attend_home(): pl.pallas_call(functools.partial(forward_home_kernel, cols, len(shards)),...  78.5 us
    pallas_call x1, Pallas kernels, reduce_all(): pl.pallas_call(functools.partial(reduce_kernel, depths, count), out_shape...  29.8 us
    pallas_call x1, Pallas kernels, gather_all(): pl.pallas_call(functools.partial(gather_kernel, depths, count), out_shape...  29.2 us
    pallas_call x1, Pallas kernels, project(): pl.pallas_call(functools.partial(project_kernel, cols), out_shape=[jax.Sh...  25.5 us
    unnamed x55, local copies, waits for them, and re-layouts  22.8 us
    dot_general x15, matrix products, dot(): lax.dot_general(left, right, (((over[0],), (over[1],)), ((), ())), prefer...  20.4 us

profile of v2, /device:TPU:0, one launch (start us, length us, event | category | flops | bytes accessed | tf_op | source)
XLA Modules:
  0.0 494.5 jit_solution(11834932248778180855)
XLA Ops:
  6.8 1.5 pad_maximum_fusion.6.refs_0_
  11.0 29.2 %shard_map.297 = (bf16[2,4,2,2,24,2304]{5,4,3,2,1,0:T(8,128)(2,1)}, f32[2,4,2,2,8,128]{5,4,3,2,1,0:T(8,128)}) custom-call(bf16[24,2304]{1,0:T(8,128)(2,1)} %pad_maximum_fusion.6.refs_0_, f32[8,128]{1,0:T(8,128)} %bitcast.160), custom_call_target="tpu_custom_call" | custom-call | tf_op jit(solution)/shard_map/pallas_call | solution.py:518
  40.3 1.5 slice_reduce_fusion.2
  45.6 2.0 copy-done.3
  47.6 25.5 %shard_map.298 = (bf16[256,768]{1,0:T(8,128)(2,1)S(1)}, f32[256,1]{1,0:T(8,128)S(1)}, bf16[16,64,256]{2,1,0:T(8,128)(2,1)S(1)}, bf16[32,128,256]{2,1,0:T(8,128)(2,1)S(1)}) custom-call(f32[256,768]{1,0:T(8,128)S(1)} %bitcast.125, f32[1,768]{1,0:T(1,128)S(1)} %reshape_reshape_squeeze.3.gain_ref, bf16[768,2304]{1,0:T(8,128)(2,1)S(1)} %bitcast.123, ...), custom_call_target="tpu_custom_call" | custom-call | tf_op jit(solution)/shard_map/pallas_call | solution.py:990
  74.1 78.5 %shard_map.299 = (f32[16,64,256]{2,1,0:T(8,128)S(1)}, f32[16,1,256]{2,1,0:T(1,128)S(1)}, bf16[12,64,256]{2,1,0:T(8,128)(2,1)S(1)}, bf16[2,4,2,2,24,768]{5,4,3,2,...) custom-call(bf16[16,64,256]{2,1,0:T(8,128)(2,1)S(1)} %get-tuple-element.53.refs_0_,, ...), custom_call_target="tpu_custom_call" | custom-call | tf_op jit(solution)/shard_map/pallas_call | solution.py:1366
  154.7 1.8 convolution_convert_fusion.1
  156.5 76.9 %shard_map.300 = (bf16[16,64,768]{2,1,0:T(8,128)(2,1)}, bf16[16,2,64,768]{3,2,1,0:T(8,128)(2,1)}, bf16[4,512,1024]{2,1,0:T(8,128)(2,1)}, bf16[4,512,1024]{2,1,0:...) custom-call(bf16[16,64,768]{2,1,0:T(8,128)(2,1)} %bitcast.147, ...), custom_call_target="tpu_custom_call" | custom-call | tf_op jit(solution)/shard_map/pallas_call | solution.py:1919
  233.4 2.2 fusion.5
  235.6 2.8 fusion.7
  238.8 1.7 copy.78
  242.4 1.8 add_convert_fusion
  244.3 77.1 %shard_map.301 = (bf16[16,64,768]{2,1,0:T(8,128)(2,1)}, f32[768,1024]{1,0:T(8,128)}, f32[768,1024]{1,0:T(8,128)}, f32[1024,768]{1,0:T(8,128)}, bf16[768,4096]{1,...) custom-call(bf16[16,64,768]{2,1,0:T(8,128)(2,1)} %bitcast.138, bf16[768,1024]{1,0:T(8,128)(2,1)} %refs_1_.3, ...), custom_call_target="tpu_custom_call" | custom-call | tf_op jit(solution)/shard_map/pallas_call | solution.py:1919
  321.4 2.1 fusion.9
  326.0 1.5 convolution_convert_fusion.2
  327.5 111.9 %shard_map.302 = (bf16[12,64,256]{2,1,0:T(8,128)(2,1)S(1)}, bf16[12,128,256]{2,1,0:T(8,128)(2,1)}, f32[24,4096]{1,0:T(8,128)S(1)}, f32[64,768]{1,0:T(8,128)S(1)}, f32[24,768]{1,0:T(8,128)S(1)}) custom-call(bf16[16,64,256]{2,1,0:T(8,128)(2,1)S(1)} %copy-done.6, bf16[32,128,256]{2,1,0:T(8,128)(2,1)} %copy-done, f32[16,64,256]{2,1,0:T(8,128)} %copy-done.7, ...), custom_call_target="tpu_custom_call" | custom-call | tf_op jit(solution)/shard_map/pallas_call | solution.py:1651
  441.5 1.4 copy-done.4
  444.4 1.7 copy.79
  446.2 3.9 convolution_convert_fusion
  450.1 29.8 %shard_map.303 = (f32[24,2304]{1,0:T(8,128)S(1)}, f32[8,128]{1,0:T(8,128)S(1)}) custom-call(bf16[2,4,2,2,24,2304]{5,4,3,2,1,0:T(8,128)(2,1)} %bitcast.141, f32[2,4,2,2,8,128]{5,4,3,2,1,0:T(8,128)S(1)} %bitcast.129), custom_call_target="tpu_custom_call" | custom-call | tf_op jit(solution)/shard_map/pallas_call | solution.py:720
  484.4 4.1 copy.113
  488.5 1.7 copy.114
  490.1 1.4 copy-done.16
  491.5 1.7 copy.115
  (121 shorter events, 26.2 us)
Async XLA Ops:
  0.6 10.3 %copy-start.15 = (f32[256,1,768]{2,1,0:T(1,128)S(1)}, f32[256,1,768]{2,1,0:T(1,128)}, u32[]{:S(2)}) copy-start(f32[256,1,768]{2,1,0:T(1,128)} %param.18) | copy-start | bytes 2359300
  45.4 28.7 %copy-start.8 = (bf16[64,768]{1,0:T(8,128)(2,1)S(1)}, bf16[64,768]{1,0:T(8,128)(2,1)}, u32[]{:S(2)}) copy-start(bf16[64,768]{1,0:T(8,128)(2,1)} %refs_4_.1) | copy-start | bytes 294916
  45.4 28.7 %copy-start.9 = (bf16[24,768]{1,0:T(8,128)(2,1)S(1)}, bf16[24,768]{1,0:T(8,128)(2,1)}, u32[]{:S(2)}) copy-start(bf16[24,768]{1,0:T(8,128)(2,1)} %refs_3_.3) | copy-start | bytes 110596
  45.6 2.0 copy-start.3
  73.2 0.8 copy-start.10
  73.9 79.3 %copy-start = (bf16[32,128,256]{2,1,0:T(8,128)(2,1)}, bf16[32,128,256]{2,1,0:T(8,128)(2,1)S(1)}, u32[]{:S(2)}) copy-start(bf16[32,128,256]{2,1,0:T(8,128)(2,1)S(1)} %get-tuple-element.54.refs_1_) | copy-start | bytes 6291460
  73.9 79.3 %copy-start.5 = (bf16[16,64,256]{2,1,0:T(8,128)(2,1)}, bf16[16,64,256]{2,1,0:T(8,128)(2,1)S(1)}, u32[]{:S(2)}) copy-start(bf16[16,64,256]{2,1,0:T(8,128)(2,1)S(1)} %get-tuple-element.53.refs_0_) | copy-start | bytes 1572868
  152.6 1.9 copy-start.1
  152.6 1.9 copy-start.7
  153.2 1.0 copy-start.12
  233.4 2.2 copy-start.13
  233.4 2.2 copy-start.18
  321.4 2.1 copy-start.14
  324.1 1.3 copy-start.2
  325.4 2.1 copy-start.6
  439.4 1.3 copy-start.19
  440.7 0.7 copy-start.20
  440.8 2.1 copy-start.4
  444.2 2.1 copy-start.11
  484.4 4.1 copy-start.17
  488.5 3.0 copy-start.16

commit v3 on v2

--- a/solution.py
+++ b/solution.py
@@ -130,7 +130,7 @@
     def scratch(self):
         held = self.arrays + [self.out_shape[i] for i in self.own_buffers()]
         total = len(self.arrays) + len(self.out_shape)
-        return [pltpu.VMEM(a.shape, a.dtype) for a in held] + [pltpu.SemaphoreType.DMA((total,))]
+        return [pltpu.VMEM(a.shape, a.dtype) for a in held] + [pltpu.SemaphoreType.DMA((max(total, 1),))]
 
     def bind(self, refs):
         count, total = len(self.arrays), len(self.arrays) + len(self.out_shape)
@@ -497,6 +497,78 @@
         loop(0, self.depths, step)
 
 
+class DepthGather:
+    def __init__(self, source, result, sems, depths):
+        self.source, self.result, self.sems, self.depths = source, result, sems, depths
+
+    def along(self, s):
+        head, depth, x, core = spot()
+        device = at_spot(head, lax.rem(depth + s, self.depths), x, core)
+        return push(
+            self.source, self.result.at[depth], self.sems[0].at[s], self.sems[1].at[s], device
+        )
+
+    def own(self):
+        return pltpu.make_async_copy(self.source, self.result.at[spot()[1]], self.sems[2])
+
+    def start(self):
+        self.own().start()
+        loop(1, self.depths, lambda s: self.along(s).start())
+
+    def finish(self):
+        self.own().wait()
+        loop(1, self.depths, lambda s: self.along(s).wait())
+
+
+def depth_sems(depths):
+    return [pltpu.SemaphoreType.DMA((depths,))] * 2 + [pltpu.SemaphoreType.DMA]
+
+
+class PlaneGather(Gather):
+    def near_copy(self, s, device, send_sem, recv_sem):
+        head, depth, x, core = spot()
+        goal = lax.rem(depth - s + self.depths, self.depths)
+        target = self.result.at[head, goal, x, core]
+        return push(self.source.at[goal], target, send_sem, recv_sem, device)
+
+    def hop(self, kind, s):
+        if kind > 1:
+            return super().hop(kind, s)
+        head, depth, x, core = spot()
+        device = at_spot(head, depth, 1 - x, core) if kind == 0 else at_spot(1 - head, depth, x, core)
+        return self.near_copy(
+            s, device, self.sems[2 + 2 * kind].at[s], self.sems[3 + 2 * kind].at[s]
+        )
+
+    def share(self, part, s):
+        if part > 0:
+            return super().share(part, s)
+        head, depth, x, core = spot()
+        device = at_spot(head, depth, x, 1 - core)
+        return self.near_copy(s, device, self.sems[10].at[part, s], self.sems[11].at[part, s])
+
+    def own(self):
+        head, _, x, core = spot()
+        return pltpu.make_async_copy(
+            self.source, self.result.at[head, :, x, core], self.sems[12]
+        )
+
+    def start(self):
+        self.own().start()
+        loop(0, self.depths, self.begin_near)
+
+    def finish(self):
+        self.own().wait()
+
+        def step(s):
+            for kind in (0, 1) + self.kinds():
+                self.hop(kind, s).wait_send()
+            for part in range(4):
+                self.share(part, s).wait()
+
+        loop(0, self.depths, step)
+
+
 def cut_of(width):
     return width // 256 * 128 if width >= 256 else width
 
@@ -870,8 +942,8 @@
 
 
 def project_kernel(
-    cols, x_ref, gain_ref, w_ref, cos_ref, sin_ref, normed_ref, scale_ref, q_out, kv_out,
-    stage, q_send, q_recv, kv_send, kv_recv, fwd_send, fwd_recv, own_sem,
+    cols, x_ref, gain_ref, cos_ref, sin_ref, w_far, normed_ref, scale_ref, q_out, kv_out,
+    stage, w_ref, q_send, q_recv, kv_send, kv_recv, fwd_send, fwd_recv, own_sem,
 ):
     me = flat_index(cols)
     core, pair = lax.rem(me, 2), lax.div(me, 2)
@@ -880,6 +952,8 @@
     pairs, heads = q_out.shape[0], stage.shape[0]
     barrier = pltpu.get_barrier_semaphore()
     width = heads * HEAD_DIM
+    weights = pltpu.make_async_copy(w_far, w_ref, own_sem.at[2])
+    weights.start()
 
     @pl.when(holds)
     def _():
@@ -914,6 +988,7 @@
         block = kv_out.at[source * 2 + core]
         return remote(block, block, fwd_send.at[source], fwd_recv.at[source], sibling, cols)
 
+    weights.wait()
     per = TILE // HEAD_DIM
     for group in range(heads // per):
         for part in range(3):
@@ -995,22 +1070,23 @@
             jax.ShapeDtypeStruct((pairs, HEAD_DIM, tokens), jnp.bfloat16),
             jax.ShapeDtypeStruct((2 * pairs, 2 * HEAD_DIM, tokens), jnp.bfloat16),
         ],
-        in_specs=[vmem] * 5,
+        in_specs=[vmem] * 4 + [everywhere],
         out_specs=[vmem, vmem, everywhere, everywhere],
         scratch_shapes=[
             pltpu.VMEM((heads, 3 * HEAD_DIM, tokens), jnp.bfloat16),
+            pltpu.VMEM(weights.shape, weights.dtype),
             by_unit,
             by_pair,
             by_unit,
             by_pair,
             by_pair,
             by_pair,
-            pltpu.SemaphoreType.DMA((2,)),
+            pltpu.SemaphoreType.DMA((3,)),
         ],
         compiler_params=pltpu.CompilerParams(
             collective_id=collective_id, has_side_effects=True, vmem_limit_bytes=40 * 2**20
         ),
-    )(rows, gain.reshape(1, width), weights, cosine, sine)
+    )(rows, gain.reshape(1, width), cosine, sine, weights)
 
 
 def to_tokens_kernel(cols, pairs, with_kv, *refs):
@@ -1286,16 +1362,21 @@
     ]
 
 
-GATHER_AT = {"start": 0, "start_own": 0, "spread_near": 8, "spread_far": 11, "settle": 14}
-
-
-def forward_home_kernel(cols, count, *refs):
+GATHER_AT = {"start": 0, "start_own": 0, "spread_near": 8, "spread_far": 12, "settle": 15}
+
+
+def forward_home_kernel(cols, count, deep, *refs):
     q_ref, kv_ref, run_ref = refs[:3]
-    sources, refs = refs[3 : 3 + count], refs[3 + count :]
+    sources, refs = refs[3 : 3 + count + deep], refs[3 + count + deep :]
     o_ref, lse_ref, home = refs[:3]
-    results, refs = refs[3 : 3 + count], refs[3 + count :]
+    results, refs = refs[3 : 3 + count + deep], refs[3 + count + deep :]
     key_rows, kept, low, send, recv, own_sem = refs[:6]
-    gathers = gathers_of(sources, results, refs[6:], cols // 4)
+    refs, deep_sems = refs[6 : 6 + GATHER_SEMS * count], refs[6 + GATHER_SEMS * count :]
+    gathers = gathers_of(sources[:count], results[:count], refs, cols // 4)
+    depth_gathers = [
+        DepthGather(sources[count + i], results[count + i], deep_sems[3 * i : 3 * i + 3], cols // 4)
+        for i in range(deep)
+    ]
     tile, tiles = pl.program_id(0), tiles_of(kv_ref)
     me, core, pair, holds, unit = my_unit()
 
@@ -1319,6 +1400,11 @@
             for gather in gathers:
                 getattr(gather, name)()
 
+    @pl.when(tile == GATHER_AT["spread_near"])
+    def _():
+        for gather in depth_gathers:
+            gather.start()
+
     def away(t):
         return remote(
             low.at[t], home.at[unit], send.at[t], recv.at[unit], t * 2 + core, cols
@@ -1336,7 +1422,7 @@
 
     @pl.when(tile == tiles - 1)
     def _():
-        for gather in gathers:
+        for gather in gathers + depth_gathers:
             gather.finish()
 
         def arrived(u, holder):
@@ -1359,15 +1445,15 @@
     return kv_ref.shape[0] // 2
 
 
-def attend_home(queries, keys_values, run, shards, cols, collective_id):
+def attend_home(queries, keys_values, run, shards, deep, cols, collective_id):
     tiles, units, depths = queries.shape[0], queries.shape[0] // 4 * 3, cols // 4
     held = pl.BlockSpec(keys_values.shape, lambda i: (0, 0, 0))
     everywhere = pl.BlockSpec(memory_space=pl.ANY)
     return pl.pallas_call(
-        functools.partial(forward_home_kernel, cols, len(shards)),
+        functools.partial(forward_home_kernel, cols, len(shards), len(deep)),
         grid=(tiles,),
-        in_specs=[tile_spec(HEAD_DIM), held, tile_spec(1)] + [everywhere] * len(shards),
-        out_specs=[tile_spec(HEAD_DIM), tile_spec(1), everywhere] + [everywhere] * len(shards),
+        in_specs=[tile_spec(HEAD_DIM), held, tile_spec(1)] + [everywhere] * (len(shards) + len(deep)),
+        out_specs=[tile_spec(HEAD_DIM), tile_spec(1), everywhere] + [everywhere] * (len(shards) + len(deep)),
         scratch_shapes=forward_scratch(keys_values.shape[0])
         + [
             pltpu.VMEM((tiles, HEAD_DIM, TILE), jnp.bfloat16),
@@ -1375,17 +1461,19 @@
             pltpu.SemaphoreType.DMA((units,)),
             pltpu.SemaphoreType.DMA,
         ]
-        + gather_sems(depths) * len(shards),
+        + gather_sems(depths) * len(shards)
+        + depth_sems(depths) * len(deep),
         out_shape=[
             jax.ShapeDtypeStruct((tiles, HEAD_DIM, TILE), jnp.float32),
             jax.ShapeDtypeStruct((tiles, 1, TILE), jnp.float32),
             jax.ShapeDtypeStruct((units, HEAD_DIM, TILE), jnp.bfloat16),
         ]
-        + [gathered_shape(shard, depths) for shard in shards],
+        + [gathered_shape(shard, depths) for shard in shards]
+        + [jax.ShapeDtypeStruct((depths,) + shard.shape, shard.dtype) for shard in deep],
         compiler_params=pltpu.CompilerParams(
             collective_id=collective_id, has_side_effects=True, vmem_limit_bytes=48 * 2**20
         ),
-    )(queries, keys_values, run, *shards)
+    )(queries, keys_values, run, *shards, *deep)
 
 
 def backward_tile(
@@ -1773,12 +1861,14 @@
 
 
 def expert_kernel(cols, step, final, work_first, work, shapes, *refs):
-    held_in, held_out, extra = shapes
+    held_in, held_out, extra, plane = shapes
     sending, refs = refs[0], refs[1:]
+    plane_in, refs = refs[:plane], refs[plane:]
     inputs, refs = refs[:held_in], refs[held_in:]
     extra_in = len(work.arrays)
     work_in, refs = refs[:extra_in], refs[extra_in:]
     returned, refs = refs[0], refs[1:]
+    plane_out, refs = refs[:plane], refs[plane:]
     outputs, refs = refs[:held_out], refs[held_out:]
     work_out, refs = refs[: len(work.out_shape)], refs[len(work.out_shape) :]
     land, partial, inbox, refs = refs[0], refs[1], refs[2], refs[3:]
@@ -1786,6 +1876,17 @@
     back_send, back_recv, own_sem, load_sem, refs = refs[:4] + (refs[4:],)
     held, refs = refs[:held_in], refs[held_in:]
     scratch, refs = refs[:extra], refs[extra:]
+    plane_sems, refs = refs[: GATHER_SEMS * plane], refs[GATHER_SEMS * plane :]
+    planes = [
+        PlaneGather(
+            plane_in[i],
+            plane_out[i],
+            plane_sems[GATHER_SEMS * i : GATHER_SEMS * (i + 1)],
+            cols // 4,
+            cut_of(plane_in[i].shape[-1]),
+        )
+        for i in range(plane)
+    ]
     begin, run, end = work.bind(work_in + work_out + refs)
 
     me = flat_index(cols)
@@ -1852,6 +1953,8 @@
     for quarter in (order[2], order[0], order[1], order[3]):
         others(quarter, lambda e: out(e).start())
     own_in.start()
+    for gather in planes:
+        gather.start()
     own_in.wait()
     share(pair).start()
     if work_first:
@@ -1886,8 +1989,12 @@
     own_back.start()
     take(order[2])
     give(order[2])
+    for gather in planes:
+        gather.spread_far()
     take(order[3])
     give(order[3])
+    for gather in planes:
+        gather.settle()
     if not work_first:
         run()
     final(land, held, scratch, outputs)
@@ -1898,10 +2005,14 @@
         loop(0, per, lambda k: share(quarter * per + k).wait_send())
         near(quarter).wait_send()
     own_back.wait()
+    for gather in planes:
+        gather.finish()
     end()
 
 
-def expert_pass(sending, held, out_shape, extra, step, final, work, work_first, cols, collective_id):
+def expert_pass(
+    sending, held, out_shape, extra, step, final, work, work_first, cols, collective_id, plane=()
+):
     pairs, slots, width = sending.shape
     block = (pairs, slots, width)
     both = (pairs, 2, slots, width)
@@ -1912,20 +2023,22 @@
         pltpu.VMEM(block, sending.dtype),
     ]
     scratch += [sems] * 8 + [pltpu.SemaphoreType.DMA((2,)), pltpu.SemaphoreType.DMA((len(held),))]
-    scratch += [pltpu.VMEM(a.shape, a.dtype) for a in held] + extra + work.scratch()
-    out_shape = [jax.ShapeDtypeStruct(block, sending.dtype)] + out_shape
-    shapes = (len(held), len(out_shape) - 1, len(extra))
+    scratch += [pltpu.VMEM(a.shape, a.dtype) for a in held] + extra
+    scratch += gather_sems(cols // 4) * len(plane) + work.scratch()
+    shapes = (len(held), len(out_shape), len(extra), len(plane))
+    whole = [gathered_shape(jax.ShapeDtypeStruct(a.shape[1:], a.dtype), cols // 4) for a in plane]
+    out_shape = [jax.ShapeDtypeStruct(block, sending.dtype)] + whole + out_shape
     everywhere = pl.BlockSpec(memory_space=pl.ANY)
     return pl.pallas_call(
         functools.partial(expert_kernel, cols, step, final, work_first, work, shapes),
         out_shape=out_shape + work.out_shape,
-        in_specs=[everywhere] * (1 + len(held) + len(work.arrays)),
+        in_specs=[everywhere] * (1 + len(plane) + len(held) + len(work.arrays)),
         out_specs=[everywhere] * (len(out_shape) + len(work.out_shape)),
         scratch_shapes=scratch,
         compiler_params=pltpu.CompilerParams(
             collective_id=collective_id, has_side_effects=True, vmem_limit_bytes=52 * 2**20
         ),
-    )(sending, *held, *work.arrays)
+    )(sending, *plane, *held, *work.arrays)
 
 
 def forward_step(quarter, per, land, partial, held, scratch):
@@ -1957,15 +2070,15 @@
         copy.wait()
 
 
-def expert_forward(sending, gate, up, down, work, cols, collective_id):
+def expert_forward(sending, gate, up, down, plane, cols, collective_id):
     pairs, slots, width = sending.shape
     kept = (QUARTERS, 2 * pairs * slots // QUARTERS, gate.shape[1])
     out_shape = [jax.ShapeDtypeStruct((pairs, 2, slots, width), sending.dtype)]
     out_shape += [jax.ShapeDtypeStruct(kept, sending.dtype)] * 3
     extra = [pltpu.VMEM(kept, sending.dtype)] * 3 + [pltpu.SemaphoreType.DMA((4,))]
     return expert_pass(
-        sending, [gate, up, down], out_shape, extra, forward_step, forward_final, work, False,
-        cols, collective_id,
+        sending, [gate, up, down], out_shape, extra, forward_step, forward_final,
+        Work([], [], lambda ins, outs, done: None), False, cols, collective_id, plane,
     )
 
 
@@ -2137,7 +2250,7 @@
             .reshape(HEADS, rows, tokens)
         )
 
-    at_home = rows_dev == TILE and groups == 1
+    at_home = rows_dev == TILE and groups == 1 and slices == 2
     if at_home:
         normed_attn, scaling_attn, q_blocks, kv_blocks = project(
             flat_in, gain_attn, proj_mat, cosine, sine, cols, 1
@@ -2168,16 +2281,16 @@
     run = segment_starts(place, unit_lengths).reshape(-1, 1, TILE)
     queries, keys_values = to_tiles(q_blocks), to_tiles(kv_blocks)
     if at_home:
-        exact, lse, attended, out_mat, share_down, share_wide = attend_home(
-            queries, keys_values, run, [w_out, shared_down, wide], cols, 2
+        exact, lse, attended, out_mat, share_down, wide = attend_home(
+            queries, keys_values, run, [w_out, shared_down], [wide], cols, 2
         )
     else:
         exact, low, lse = attend(queries, keys_values, run, rows_dev)
         (attended,) = to_tokens([from_tiles(low, rows_dev)], cols, 2)
         out_mat, share_down, share_wide = gather_all([w_out, shared_down, wide], cols, 11)
+        share_wide = share_wide.reshape(model_width, 2 * hidden)
     out_mat = out_mat.reshape(model_width, model_width)
     share_down = share_down.reshape(hidden, model_width)
-    share_wide = share_wide.reshape(model_width, 2 * hidden)
     attended = by_head(attended).reshape(model_width, tokens)
 
     residual_mid = flat_in + dot(attended, out_mat, (0, 0))
@@ -2203,22 +2316,30 @@
     chosen = jnp.sum(route_onehot * logits[:, None, :], axis=-1)
     gate_probs = jax.nn.softmax(chosen, axis=1)
     out = jax.ShapeDtypeStruct
-    shared_work = Work(
-        [normed_ffn, share_wide, share_down],
-        [
-            out((tokens, hidden), bf16),
-            out((tokens, hidden), bf16),
-            out((tokens, hidden), bf16),
-            out((tokens, model_width), f32),
-        ],
-        shared_forward,
-    )
-    if slices == 2:
-        passed = expert_forward(
-            sending, expert_gate, expert_up, expert_down, shared_work, cols, 3
-        )
-        returned, kept, shared_results = passed[0], passed[1:5], passed[5:]
+    if at_home:
+        returned, share_wide, *kept = expert_forward(
+            sending, expert_gate, expert_up, expert_down, [wide], cols, 3
+        )
+        share_wide = share_wide.reshape(model_width, 2 * hidden)
+        shared_in = dot(normed_ffn, share_wide, (1, 0))
+        shared_hidden = (apply_silu(shared_in[:, :hidden]) * shared_in[:, hidden:]).astype(bf16)
+        shared_results = [
+            shared_in[:, :hidden].astype(bf16),
+            shared_in[:, hidden:].astype(bf16),
+            shared_hidden,
+            dot(shared_hidden, share_down, (1, 0)),
+        ]
     else:
+        shared_work = Work(
+            [normed_ffn, share_wide, share_down],
+            [
+                out((tokens, hidden), bf16),
+                out((tokens, hidden), bf16),
+                out((tokens, hidden), bf16),
+                out((tokens, model_width), f32),
+            ],
+            shared_forward,
+        )
         (arrived,) = spread([sending], cols, slices, EXPERTS, 3)
         arrived = arrived.reshape(devices * CAP, model_width)
         inner_gate = dot(arrived, expert_gate, (1, 0))
@@ -2263,7 +2384,7 @@
         {0: 5, 1: 6},
     )
     back_send = back_send.reshape(EXPERTS, CAP, model_width)
-    if slices == 2:
+    if at_home:
         passed = expert_backward(
             back_send, expert_gate, expert_up, expert_down, kept, shared_work, cols, 5
         )

time: 499 us -> 495 us (level)
  Pallas kernels: 429 us -> 406 us
  local copies, waits for them, and re-layouts: 30.1 us -> 38.7 us
  matrix products: 20.4 us -> 28 us
    pallas_call x1, Pallas kernels: 78.5 us -> 56.2 us  [attend_home(): pl.pallas_call(functools.partial(forward_home_kernel, cols, len(shards),...]
    dot_general x15 -> x17, matrix products: 20.4 us -> 28 us  [dot(): lax.dot_general(left, right, (((over[0],), (over[1],)), ((), ())), prefer...]
    unnamed x55 -> x99, local copies, waits for them, and re-layouts: 22.8 us -> 26.4 us
where the time goes in v3:
time: 495 us; the launch traced here: 490 us
  Pallas kernels  406 us (82%)
  local copies, waits for them, and re-layouts  38.7 us (8%)
  matrix products  28 us (6%)
  other arithmetic  13 us (3%)
    pallas_call x2, Pallas kernels, expert_pass(): pl.pallas_call(functools.partial(expert_kernel, cols, step, final, work_f...  154 us
    pallas_call x1, Pallas kernels, attend_back_home(): pl.pallas_call(functools.partial(backward_home_kernel, cols, depths, len(...  110 us
    pallas_call x1, Pallas kernels, attend_home(): pl.pallas_call(functools.partial(forward_home_kernel, cols, len(shards),...  56.2 us
    pallas_call x1, Pallas kernels, reduce_all(): pl.pallas_call(functools.partial(reduce_kernel, depths, count), out_shape...  29.7 us
    pallas_call x1, Pallas kernels, gather_all(): pl.pallas_call(functools.partial(gather_kernel, depths, count), out_shape...  29.2 us
    dot_general x17, matrix products, dot(): lax.dot_general(left, right, (((over[0],), (over[1],)), ((), ())), prefer...  28 us
    unnamed x99, local copies, waits for them, and re-layouts  26.4 us
    pallas_call x1, Pallas kernels, project(): pl.pallas_call(functools.partial(project_kernel, cols), out_shape=[jax.Sh...  26 us

profile of v3, /device:TPU:0, one launch (start us, length us, event | category | flops | bytes accessed | tf_op | source)
XLA Modules:
  0.0 490.0 jit_solution(275017470163190769)
XLA Ops:
  12.8 29.2 %shard_map.297 = (bf16[2,4,2,2,24,2304]{5,4,3,2,1,0:T(8,128)(2,1)}, f32[2,4,2,2,8,128]{5,4,3,2,1,0:T(8,128)}) custom-call(bf16[24,2304]{1,0:T(8,128)(2,1)} %pad_maximum_fusion.6.refs_0_, f32[8,128]{1,0:T(8,128)} %bitcast.167), custom_call_target="tpu_custom_call" | custom-call | tf_op jit(solution)/shard_map/pallas_call | solution.py:590
  47.9 2.0 copy-done.1
  49.9 26.0 %shard_map.298 = (bf16[256,768]{1,0:T(8,128)(2,1)S(1)}, f32[256,1]{1,0:T(8,128)S(1)}, bf16[16,64,256]{2,1,0:T(8,128)(2,1)S(1)}, bf16[32,128,256]{2,1,0:T(8,128)(2,1)S(1)}) custom-call(f32[256,768]{1,0:T(8,128)S(1)} %bitcast.129, f32[1,768]{1,0:T(1,128)S(1)} %reshape_reshape_squeeze.3.gain_ref, f32[32,256]{1,0:T(8,128)S(1)} %get-tuple-element.179.cos_ref, ...), custom_call_target="tpu_custom_call" | custom-call | tf_op jit(solution)/shard_map/pallas_call | solution.py:1065
  78.7 56.2 %shard_map.299 = (f32[16,64,256]{2,1,0:T(8,128)S(1)}, f32[16,1,256]{2,1,0:T(1,128)S(1)}, bf16[12,64,256]{2,1,0:T(8,128)(2,1)S(1)}, bf16[2,4,2,2,24,768]{5,4,3,2,...) custom-call(bf16[16,64,256]{2,1,0:T(8,128)(2,1)S(1)} %get-tuple-element.50.refs_0_, ...), custom_call_target="tpu_custom_call" | custom-call | tf_op jit(solution)/shard_map/pallas_call | solution.py:1452
  137.6 2.5 convolution_convert_fusion.1
  140.0 73.9 %shard_map.300 = (bf16[16,64,768]{2,1,0:T(8,128)(2,1)}, bf16[2,4,2,2,24,4096]{5,4,3,2,1,0:T(8,128)(2,1)}, bf16[16,2,64,768]{3,2,1,0:T(8,128)(2,1)}, bf16[4,512,1...) custom-call(bf16[16,64,768]{2,1,0:T(8,128)(2,1)} %bitcast.148, ...), custom_call_target="tpu_custom_call" | custom-call | tf_op jit(solution)/shard_map/pallas_call | solution.py:2032
  214.0 2.2 fusion.3
  216.9 4.7 fusion.47
  222.2 1.6 fusion.42
  224.0 1.6 copy-done.11
  225.5 2.8 multiply_reduce_fusion.5
  230.7 1.8 reshape.585
  232.5 2.8 copy.78
  236.7 1.8 add_convert_fusion
  238.5 80.2 %shard_map.301 = (bf16[16,64,768]{2,1,0:T(8,128)(2,1)}, f32[768,1024]{1,0:T(8,128)}, f32[768,1024]{1,0:T(8,128)}, f32[1024,768]{1,0:T(8,128)}, bf16[768,4096]{1,...) custom-call(bf16[16,64,768]{2,1,0:T(8,128)(2,1)} %bitcast.141, bf16[768,1024]{1,0:T(8,128)(2,1)} %refs_1_.1, ...), custom_call_target="tpu_custom_call" | custom-call | tf_op jit(solution)/shard_map/pallas_call | solution.py:2032
  318.8 2.1 fusion.10
  322.8 2.6 convolution_convert_fusion.2
  325.5 110.3 %shard_map.302 = (bf16[12,64,256]{2,1,0:T(8,128)(2,1)S(1)}, bf16[12,128,256]{2,1,0:T(8,128)(2,1)}, f32[24,4096]{1,0:T(8,128)S(1)}, f32[64,768]{1,0:T(8,128)S(1)}, f32[24,768]{1,0:T(8,128)S(1)}) custom-call(bf16[16,64,256]{2,1,0:T(8,128)(2,1)S(1)} %get-tuple-element.50.refs_0_, bf16[32,128,256]{2,1,0:T(8,128)(2,1)} %copy-done, f32[16,64,256]{2,1,0:T(8,128)} %copy-done.3, ...), custom_call_target="tpu_custom_call" | custom-call | tf_op jit(solution)/shard_map/pallas_call | solution.py:1739
  440.9 1.7 copy.79
  442.7 2.9 convolution_convert_fusion
  445.6 29.7 %shard_map.303 = (f32[24,2304]{1,0:T(8,128)S(1)}, f32[8,128]{1,0:T(8,128)S(1)}) custom-call(bf16[2,4,2,2,24,2304]{5,4,3,2,1,0:T(8,128)(2,1)} %bitcast.144, f32[2,4,2,2,8,128]{5,4,3,2,1,0:T(8,128)S(1)} %bitcast.133), custom_call_target="tpu_custom_call" | custom-call | tf_op jit(solution)/shard_map/pallas_call | solution.py:792
  479.8 4.1 copy.113
  484.0 1.7 copy.114
  487.0 1.7 copy.115
  (168 shorter events, 39.2 us)
Async XLA Ops:
  0.6 12.1 %copy-start.15 = (f32[256,1,768]{2,1,0:T(1,128)S(1)}, f32[256,1,768]{2,1,0:T(1,128)}, u32[]{:S(2)}) copy-start(f32[256,1,768]{2,1,0:T(1,128)} %param.18) | copy-start | bytes 2359300
  10.4 126.5 %copy-start.29 = (s32[256,2]{0,1:T(2,128)}, s32[256,2]{0,1:T(2,128)S(1)}, u32[]{:S(2)}) copy-start(s32[256,2]{0,1:T(2,128)S(1)} %copy.73) | copy-start | bytes 6148
  11.7 204.4 %copy-start.38 = (s32[256]{0:T(256)}, s32[256]{0:T(256)S(1)}, u32[]{:S(2)}) copy-start(s32[256]{0:T(256)S(1)} %get-tuple-element.152) | copy-start | bytes 3076
  49.9 28.7 %copy-start.4 = (bf16[64,768]{1,0:T(8,128)(2,1)S(1)}, bf16[64,768]{1,0:T(8,128)(2,1)}, u32[]{:S(2)}) copy-start(bf16[64,768]{1,0:T(8,128)(2,1)} %refs_4_.2) | copy-start | bytes 294916
  49.9 28.7 %copy-start.5 = (bf16[24,768]{1,0:T(8,128)(2,1)S(1)}, bf16[24,768]{1,0:T(8,128)(2,1)}, u32[]{:S(2)}) copy-start(bf16[24,768]{1,0:T(8,128)(2,1)} %refs_3_.3) | copy-start | bytes 110596
  78.0 56.9 %copy-start.16 = (f32[256,1,768]{2,1,0:T(1,128)S(1)}, f32[256,1,768]{2,1,0:T(1,128)}, u32[]{:S(2)}) copy-start(f32[256,1,768]{2,1,0:T(1,128)} %param.18) | copy-start | bytes 2359300
  137.6 86.3 %copy-start.24 = (f32[256,1]{0,1:T(1,128)}, f32[256,1]{0,1:T(1,128)S(1)}, u32[]{:S(2)}) copy-start(f32[256,1]{0,1:T(1,128)S(1)} %get-tuple-element.175) | copy-start | bytes 3076
  140.0 73.9 %copy-start.40 = (s32[256]{0:T(256)S(1)}, s32[256]{0:T(256)}, u32[]{:S(2)}) copy-start(s32[256]{0:T(256)} %get-tuple-element.153) | copy-start | bytes 3076
  214.0 2.2 copy-start.42
  221.5 2.4 copy-start.20
  222.2 6.1 %copy-start.14 = (bf16[256,2048]{1,0:T(8,128)(2,1)}, bf16[256,2048]{1,0:T(8,128)(2,1)S(1)}, u32[]{:S(2)}) copy-start(bf16[256,2048]{1,0:T(8,128)(2,1)S(1)} %multiply_convert_fusion.refs_12_) | copy-start | bytes 3145732
  222.2 3.3 copy-start.11
  222.2 3.3 copy-start.26
  225.5 3.4 copy-start.28
  225.5 4.1 copy-start.30
  232.5 2.9 copy-start.25
  238.5 80.3 %copy-start.39 = (s32[256]{0:T(256)S(1)}, s32[256]{0:T(256)}, u32[]{:S(2)}) copy-start(s32[256]{0:T(256)} %copy-done.38) | copy-start | bytes 3076
  318.7 2.2 copy-start.10
  318.8 2.2 copy-start.32
  437.1 2.2 copy-start.17
  437.1 2.2 copy-start.33
  437.1 2.2 copy-start.35
  479.8 4.1 copy-start.19
  484.0 3.0 copy-start.18
  (19 other events, 26.3 us)
